TPU v7x, 32 devices: a whole 2x2x4 slice. The times are simulated.
32 devices in a mesh: dp: 32 (over z, y, x, core).
Axes of the slice: x: 2, y: 2, z: 4, core: 2. Of those that a mesh axis runs over, the one named last changes fastest.
Arguments:
- view_a: bfloat16 [4096, 4096], P('dp'), may hold values from -120 to 120
- view_b: bfloat16 [4096, 4096], P('dp'), may hold values from -120 to 120
Outputs:
- loss: float32 [], replicated
- grad_a: bfloat16 [4096, 4096], P('dp')
- grad_b: bfloat16 [4096, 4096], P('dp')
All inputs are finite; a program needn't handle non-finite values.
Results may differ from a plain program's by a relative error of at most 0.0034.
Values may be sent and summed in bfloat16 or wider, within the bound.
No kernel may reach another device: no remote copies, remote signals or barrier semaphores. Data moves between devices by JAX's collectives and lax.ppermute only.
A program may use at most 192 MiB of HBM per device.

v0:
```python
import functools
import math

import jax
import jax.numpy as jnp
from jax import lax
from jax.experimental import pallas as pl
from jax.experimental.pallas import tpu as pltpu
from jax.sharding import PartitionSpec as P

lam = 0.0051
eps = 1e-05

cube = 8
orders = ((4, 2, 1), (1, 4, 2), (2, 1, 4))
together = lax.optimization_barrier
strip = 32
vmem = pl.BlockSpec(memory_space=pltpu.VMEM)
smem = pl.BlockSpec(memory_space=pltpu.SMEM)


def room(*arrays):
    sizes = [math.prod(x.shape) * x.dtype.itemsize for x in arrays]
    return pltpu.CompilerParams(vmem_limit_bytes=sum(sizes) + max(sizes) + (4 << 20))


def strips(rows, body, init=None):
    return lax.fori_loop(
        0, rows // strip, lambda i, carry: body(pl.multiple_of(i * strip, strip), carry), init
    )


def places(order):
    return [
        sum(bit for step, bit in enumerate(order) if place >> step & 1) for place in range(cube)
    ]


def cuts(width):
    part = -(-width // 384) * 128
    edges = list(range(0, width, part)) + [width]
    return list(zip(edges, edges[1:]))


def prepare_kernel(half, at_ref, a_ref, b_ref, *outs):
    near_ref, rest_ref, eighths_ref, sums_ref = outs[:4]
    rows, width = a_ref.shape
    for n in range(width // half):
        column = a_ref[:, pl.ds(pl.multiple_of(at_ref[n] * half, half), half)]
        if n < 2:
            near_ref[:, n * half : (n + 1) * half] = column
        else:
            rest_ref[:, (n - 2) * half : (n - 1) * half] = column
    parts = iter(outs[4:])
    for full_ref in (near_ref, rest_ref):
        for lo, hi in cuts(full_ref.shape[1]):
            next(parts)[...] = full_ref[:, lo:hi]
    narrow = width // cube
    for i in range(cube):
        here = slice(i * narrow, (i + 1) * narrow)
        eighths_ref[i] = b_ref[:, here]
        for n, ref in enumerate((a_ref, b_ref)):
            x = ref[:, here].astype(jnp.float32)
            sums_ref[2 * n : 2 * n + 1, here] = jnp.sum(x, axis=0, keepdims=True)
            sums_ref[2 * n + 1 : 2 * n + 2, here] = jnp.sum(x * x, axis=0, keepdims=True)


def prepare(view_a, view_b, at, half):
    rows, width = view_a.shape
    widths = [2 * half, width - 2 * half]
    shapes = [(rows, n) for n in widths] + [(cube, rows, width // cube)]
    parts = [(rows, hi - lo) for n in widths for lo, hi in cuts(n)]
    outs = [jax.ShapeDtypeStruct(shape, jnp.bfloat16) for shape in shapes]
    outs += [jax.ShapeDtypeStruct((4, width), jnp.float32)]
    outs += [jax.ShapeDtypeStruct(shape, jnp.bfloat16) for shape in parts]
    near, rest, eighths, sums, *parts = pl.pallas_call(
        functools.partial(prepare_kernel, half),
        out_shape=outs,
        in_specs=[smem, vmem, vmem],
        out_specs=[vmem] * len(outs),
        compiler_params=room(view_a, view_b, *outs),
    )(at, view_a, view_b)
    first = len(cuts(widths[0]))
    return near, rest, eighths, sums, parts[:first], parts[first:]


def double_kernel(*refs):
    n = len(refs) // 3
    for x, y, out in zip(refs[:n], refs[n : 2 * n], refs[2 * n :]):
        rows = x.shape[0]

        def body(row, _, x=x, y=y, out=out, rows=rows):
            out[pl.ds(row, strip), :] = x[pl.ds(row, strip), :]
            out[pl.ds(rows + row, strip), :] = y[pl.ds(row, strip), :]

        strips(rows, body)


def double(xs, ys):
    return pl.pallas_call(
        double_kernel,
        out_shape=[jax.ShapeDtypeStruct((2 * x.shape[0], x.shape[1]), x.dtype) for x in xs],
        in_specs=[vmem] * (2 * len(xs)),
        out_specs=[vmem] * len(xs),
        compiler_params=room(*xs, *ys, *xs, *ys),
    )(*xs, *ys)


def merge_kernel(orders, mean_ref, inv_ref, *refs):
    pieces, out_ref = refs[:-1], refs[-1]
    rows = pieces[0].shape[0] * 2 // cube
    start = 0
    for n, order in enumerate(orders[: len(pieces) // 2]):
        size = pieces[2 * n].shape[1]
        mean, inv = mean_ref[:, start : start + size], inv_ref[:, start : start + size]
        for m, r in enumerate(places(order)):
            piece, first = pieces[2 * n + 2 * m // cube], m % (cube // 2) * rows


            def body(row, _, piece=piece, first=first, r=r, start=start, size=size, mean=mean, inv=inv):
                raw = piece[pl.ds(first + row, strip), :].astype(jnp.float32)
                out_ref[pl.ds(r * rows + row, strip), start : start + size] = (
                    (raw - mean) * inv
                ).astype(jnp.bfloat16)

            strips(rows, body)
        start += size


def merge(moving, arrived, orders, mean, inv):
    pieces = [x for pair in zip(moving, arrived) for x in pair]
    return pl.pallas_call(
        functools.partial(merge_kernel, orders),
        out_shape=jax.ShapeDtypeStruct((2 * pieces[0].shape[0], mean.shape[1]), jnp.bfloat16),
        in_specs=[vmem] * (2 + len(pieces)),
        out_specs=vmem,
        compiler_params=room(*pieces, *pieces),
    )(mean, inv, *pieces)


def moments_kernel(orders, mean_ref, inv_ref, *refs):
    pieces, out_ref = refs[:-1], refs[-1]
    start = 0
    for n in range(len(pieces) // 2):
        size = pieces[2 * n].shape[1]
        here = slice(start, start + size)
        mean, inv = mean_ref[:, here], inv_ref[:, here]
        total = [jnp.zeros((8, size), jnp.float32)] * 4
        for piece in pieces[2 * n : 2 * n + 2]:

            def body(row, total, piece=piece, mean=mean, inv=inv):
                raw = piece[pl.ds(row, strip), :].astype(jnp.float32)
                flat = (raw - mean) * inv
                norm = flat.astype(jnp.bfloat16).astype(jnp.float32)
                terms = (flat, flat * norm, norm * norm, norm)
                return [
                    t + sum(x[m : m + 8, :] for m in range(0, strip, 8))
                    for t, x in zip(total, terms)
                ]

            total = strips(piece.shape[0], body, total)
        total = [jnp.sum(x, axis=0, keepdims=True) for x in total]
        out_ref[:, here] = jnp.concatenate(total, 0)
        start += size


def moments(moving, arrived, orders, mean, inv):
    pieces = [x for pair in zip(moving, arrived) for x in pair]
    return pl.pallas_call(
        functools.partial(moments_kernel, orders),
        out_shape=jax.ShapeDtypeStruct((4, mean.shape[1]), jnp.float32),
        in_specs=[vmem] * (2 + len(pieces)),
        out_specs=vmem,
        compiler_params=room(*pieces),
    )(mean, inv, *pieces)


def arrange_kernel(k_ref, blocks_ref, mean_ref, inv_ref, raw_ref, norm_ref):
    rows = blocks_ref.shape[1]
    for r in range(cube):

        def body(row, _, r=r):
            raw = blocks_ref[k_ref[0] ^ r, pl.ds(row, strip), :]
            raw_ref[pl.ds(r * rows + row, strip), :] = raw
            norm_ref[pl.ds(r * rows + row, strip), :] = (
                (raw.astype(jnp.float32) - mean_ref[...]) * inv_ref[...]
            ).astype(jnp.bfloat16)

        strips(rows, body)


def arrange(blocks, mean, inv, k):
    _, rows, n = blocks.shape
    out = jax.ShapeDtypeStruct((cube * rows, n), jnp.bfloat16)
    return pl.pallas_call(
        arrange_kernel,
        out_shape=(out, out),
        in_specs=[smem] + [vmem] * 3,
        out_specs=(vmem, vmem),
        compiler_params=room(blocks, out, out),
    )(k.reshape(1), blocks, mean, inv)


def finish_kernel(k_ref, grad_ref, raw_ref, mean_ref, inv_ref, first_ref, second_ref, out_ref):
    rows = out_ref.shape[1]
    mean, inv = mean_ref[...], inv_ref[...]
    for r in range(cube):

        def body(row, _, r=r):
            here = pl.ds(r * rows + row, strip)
            flat = (raw_ref[here, :].astype(jnp.float32) - mean) * inv
            out = inv * (grad_ref[here, :] - first_ref[...] - flat * second_ref[...])
            out_ref[k_ref[0] ^ r, pl.ds(row, strip), :] = out.astype(jnp.bfloat16)

        strips(rows, body)


def finish(grad, raw, mean, inv, first, second, k):
    size, n = grad.shape
    return pl.pallas_call(
        finish_kernel,
        out_shape=jax.ShapeDtypeStruct((cube, size // cube, n), jnp.bfloat16),
        in_specs=[smem] + [vmem] * 6,
        out_specs=vmem,
        compiler_params=room(grad, raw, raw),
    )(k.reshape(1), grad, raw, mean, inv, first, second)


def place_kernel(at_ref, *refs):
    blocks, out_ref = refs[:-1], refs[-1]
    half = blocks[0].shape[1] // 2
    for n, block in enumerate(blocks):
        for side in range(2):
            start = pl.multiple_of(at_ref[2 * n + side] * half, half)
            out_ref[:, pl.ds(start, half)] = block[:, side * half : (side + 1) * half]


def place(blocks, at):
    rows, n = blocks[0].shape
    return pl.pallas_call(
        place_kernel,
        out_shape=jax.ShapeDtypeStruct((rows, n * len(blocks)), jnp.bfloat16),
        in_specs=[smem] + [vmem] * len(blocks),
        out_specs=vmem,
        compiler_params=room(*blocks, *blocks),
    )(at, *blocks)


def dot(x, y, contract):
    return lax.dot_general(x, y, (contract, ((), ())), preferred_element_type=jnp.float32)


def cross_kernel(side, orders, k_ref, rows_ref, *refs):
    if side == 0:
        pieces, out_ref = refs[:-1], refs[-1]
    else:
        total_ref, raw_ref, mean_ref, inv_ref, first_ref, second_ref, *pieces, out_ref = refs
    narrow = rows_ref.shape[1] // cube
    start = 0
    for order, piece in zip(orders, pieces):
        here = slice(start, start + piece.shape[1])
        start += piece.shape[1]
        total = 0.0 if side == 0 else total_ref[:, here]
        for m in range(cube // 2):
            r = places(order)[side * cube // 2 + m]
            at = pl.multiple_of((k_ref[0] ^ r) * narrow, narrow)
            total = total + jnp.dot(
                rows_ref[:, pl.ds(at, narrow)],
                piece[m * narrow : (m + 1) * narrow, :],
                preferred_element_type=jnp.float32,
            )
        if side == 0:
            out_ref[:, here] = total
        else:
            inv = inv_ref[:, here]
            flat = (raw_ref[:, here].astype(jnp.float32) - mean_ref[:, here]) * inv
            out = inv * (total - first_ref[:, here] - flat * second_ref[:, here])
            out_ref[:, here] = out.astype(jnp.bfloat16)


def cross_products(side, rows, pieces, orders, k, *more):
    size, n = rows.shape[0], sum(x.shape[1] for x in pieces)
    block = min(size, 512)

    def whole(x):
        return pl.BlockSpec(x.shape, lambda i: (0, 0))

    def part(x):
        return pl.BlockSpec((block, x.shape[1]), lambda i: (i, 0))

    out = jax.ShapeDtypeStruct((size, n), jnp.bfloat16 if side else jnp.float32)
    specs = [part(x) if x.shape[0] == size else whole(x) for x in more]
    return pl.pallas_call(
        functools.partial(cross_kernel, side, orders),
        grid=(size // block,),
        out_shape=out,
        in_specs=[smem, part(rows)] + specs + [whole(x) for x in pieces],
        out_specs=part(out),
        cost_estimate=pl.CostEstimate(
            flops=size * n * rows.shape[1], bytes_accessed=16 * size * n, transcendentals=0
        ),
        compiler_params=pltpu.CompilerParams(vmem_limit_bytes=48 << 20),
    )(k.reshape(1), rows, *more, *pieces)


def shards(view_a, view_b):
    f32, bf16 = jnp.float32, jnp.bfloat16
    rows, width = view_a.shape
    devices = lax.axis_size("dp")
    count = rows * devices
    cubes = devices // (2 * cube)
    index = lax.axis_index("dp")
    c, k, h = index % 2, index // 2 % cube, index // (2 * cube)
    wide, half, narrow = width // cubes, width // cubes // 2, width // cube
    groups = [
        [(g * cube + i) * 2 + core for i in range(cube)] for g in range(cubes) for core in range(2)
    ]

    def swap(x, mask):
        return lax.ppermute(x, "dp", [(i, i ^ mask) for i in range(devices)])

    def swap_k(x, bit):
        return swap(x, 2 * bit)

    def turn(x, step):
        return lax.ppermute(
            x, "dp", [(i, (i + 2 * cube * step) % devices) for i in range(devices)]
        )

    def turns(x):
        return [turn(x, s) for s in range(1, cubes)]

    def exchange(x):
        return lax.all_to_all(
            x, "dp", split_axis=0, concat_axis=0, axis_index_groups=groups, tiled=True
        )

    def columns(x, start, size):
        return lax.dynamic_slice_in_dim(x, start, size, axis=1)

    at = [(h + s) % cubes * 2 + core for s in range(cubes) for core in (c, 1 - c)]

    h_masks = [2 * cube << bit for bit in range(cubes.bit_length() - 1)]

    def by_place(x, sides):
        return jnp.concatenate([columns(x, place * half, half) for place in sides], 1)

    def send(moving, step):
        return [swap_k(x, order[step]) for x, order in zip(moving, orders)]

    whole_near, whole_rest, eighths, sums, near, rest = prepare(view_a, view_b, jnp.stack(at), half)
    parts_a = [whole_near] + [whole_rest[:, s * wide : (s + 1) * wide] for s in range(cubes - 1)]
    cuts_b = (0, rows // 2, rows)
    pieces_b = [view_b[lo:hi] for lo, hi in zip(cuts_b, cuts_b[1:])]
    others_b = []

    arrived = send(rest, 0)

    own_b = exchange(eighths)
    far_1 = [turn(x[:, half:], s + 1) for s, x in enumerate(parts_a[1:])]
    for mask in [1] + h_masks:
        sums = sums + swap(sums, mask)
    rest, arrived, sums, pieces_b, near, parts_a, far_1 = together(
        (rest, arrived, sums, pieces_b, near, parts_a, far_1)
    )
    rest = double(rest, arrived)
    arrived = send(rest, 1)
    others_b.append(turns(pieces_b[0]))
    for mask in (2, 4):
        sums = sums + swap(sums, mask)
    rest, arrived, others_b, sums, pieces_b, own_b, parts_a, far_1 = together(
        (rest, arrived, others_b, sums, pieces_b, own_b, parts_a, far_1)
    )
    rest = double(rest, arrived)
    arrived = send(rest, 2)
    others_b.append(turns(pieces_b[1]))
    sums = sums + swap(sums, 8)
    means = sums / count
    mean_a, mean_b = means[0:1], means[2:3]
    inv_a = 1.0 / jnp.sqrt(means[1:2] - mean_a * mean_a + eps)
    inv_b = 1.0 / jnp.sqrt(means[3:4] - mean_b * mean_b + eps)
    mean_bn = columns(mean_b, k * narrow, narrow)
    inv_bn = columns(inv_b, k * narrow, narrow)
    mean_ap, inv_ap = by_place(mean_a, at), by_place(inv_a, at)
    near_b, right = arrange(own_b, mean_bn, inv_bn, k)
    rest, arrived, others_b, near_b, right, mean_ap, inv_ap, parts_a, far_1 = together(
        (rest, arrived, others_b, near_b, right, mean_ap, inv_ap, parts_a, far_1)
    )

    def product(left, s):
        first = dot(right, left[:, s * wide + half : (s + 1) * wide], ((0,), (0,)))
        return swap(first, 1) + dot(right, left[:, s * wide : s * wide + half], ((0,), (0,)))

    def diagonal(s):
        return (
            lax.broadcasted_iota(jnp.int32, (narrow, half), 1) + at[2 * s] * half
            == lax.broadcasted_iota(jnp.int32, (narrow, half), 0) + k * narrow
        )

    raw_rest = (rest, arrived)
    rest = merge(rest, arrived, orders, mean_ap[:, wide:], inv_ap[:, wide:])
    arrived = send(near, 0)
    partials = [product(rest, s) for s in range(cubes - 1)]
    exact = [
        jnp.sum(jnp.where(diagonal(s + 1), x, 0.0), axis=1).reshape(1, narrow)
        for s, x in enumerate(partials)
    ]
    partials = [x.astype(bf16) for x in partials]
    partials, exact, near, arrived, others_b, raw_rest, near_b = together(
        (partials, exact, near, arrived, others_b, raw_rest, near_b)
    )
    near = double(near, arrived)

    cuts_p = (0, 3 * narrow // 8, 7 * narrow // 8, narrow)
    received = []
    for step in (1, 2):
        arrived = send(near, step)
        received.append(
            [turn(x[cuts_p[step - 1] : cuts_p[step]], s + 1) for s, x in enumerate(partials)]
        )
        if step == 1:
            other_a = swap(jnp.concatenate([parts_a[0][:, half:]] + far_1, 0), 1)
            flat_b = (near_b.astype(f32) - mean_bn) * inv_bn
            wide_b = flat_b.astype(bf16).astype(f32)
            sums_b = jnp.stack(
                [jnp.sum(x, axis=0) for x in (flat_b, flat_b * wide_b, wide_b * wide_b, wide_b)]
            )
            sums_b = sums_b + swap(sums_b, 1)
            sums_a = moments(*raw_rest, orders, mean_ap[:, wide:], inv_ap[:, wide:])
            near, arrived, received, partials, exact, others_b, other_a, sums_a, sums_b = together(
                (near, arrived, received, partials, exact, others_b, other_a, sums_a, sums_b)
            )
            near = double(near, arrived)
        else:
            others_b = [jnp.concatenate(pieces, 0) for pieces in zip(*others_b)]
            pair_b = jnp.concatenate([view_b] + others_b, 0)
            pair_b = ((pair_b.astype(f32) - mean_b) * inv_b).astype(bf16)
            far_sums = [
                turn(jnp.concatenate([sums_a[:, s * wide : (s + 1) * wide], sums_b], 1), s + 1)
                for s in range(cubes - 1)
            ]
            near, arrived, received, partials, exact, pair_b, far_sums = together(
                (near, arrived, received, partials, exact, pair_b, far_sums)
            )
            sums_a = sum(x[:, :wide] for x in far_sums)
            sums_b = sums_b + sum(x[:, wide:] for x in far_sums)
    received.append([turn(x[cuts_p[2] :], s + 1) for s, x in enumerate(partials)])
    exact = [turn(x, s + 1) for s, x in enumerate(exact)]
    raw_near = (near, arrived)
    near = merge(near, arrived, orders, mean_ap[:, :wide], inv_ap[:, :wide])
    norm_b = jnp.concatenate([pair_b, swap(pair_b, 1)], 0)
    corr = product(near, 0)
    corr, received, exact, norm_b, raw_near = together(
        (corr, received, exact, norm_b, raw_near)
    )
    diag = diagonal(0)
    for blocks, line in zip(zip(*received), exact):
        block = jnp.concatenate(blocks, 0).astype(f32)
        corr = corr + jnp.where(diag, line.reshape(narrow, 1), block)
    corr = corr / count
    loss = jnp.sum(jnp.where(diag, (1.0 - corr) ** 2, lam * corr * corr))
    gcorr = jnp.where(diag, 2.0 * (corr - 1.0), 2.0 * lam * corr).astype(bf16)

    def line(sums):
        spread = sums[2:3] - sums[3:4] * sums[3:4] / count
        usable = spread > 1e-3 * sums[2:3]
        slope = jnp.where(
            usable,
            (sums[1:2] - sums[0:1] * sums[3:4] / count) / jnp.where(usable, spread, 1.0),
            1.0,
        )
        return slope, (sums[0:1] - slope * sums[3:4]) / count

    stats_a = jnp.stack(
        [
            jnp.sum(gcorr.astype(f32) * sums_b[3].reshape(narrow, 1), axis=0),
            jnp.sum(gcorr.astype(f32) * corr, axis=0),
            jnp.full((half,), loss),
        ]
    )

    moving = [gcorr[:, lo:hi] for lo, hi in cuts(half)]
    cuts_g = (0, 3 * narrow // 8, 3 * narrow // 4, narrow)
    mean_ah, inv_ah = mean_ap[:, :half], inv_ap[:, :half]
    turned, sibling = [], []
    for step in range(3):
        arrived = send(moving, step)
        piece = gcorr[cuts_g[step] : cuts_g[step + 1]]
        if step < 2:
            turned.append(turns(piece))
        else:
            both = [
                turn(jnp.concatenate([piece, x[:, :half]], 0), s + 1)
                for s, x in enumerate(parts_a[1:])
            ]
            turned.append([x[: narrow // 4] for x in both])
            far_0 = [x[narrow // 4 :] for x in both]
        if step == 0:
            for bit in (1, 2):
                stats_a = stats_a + swap_k(stats_a, bit)
            sums_a = sums_a + moments(*raw_near, orders, mean_ap[:, :wide], inv_ap[:, :wide])
            moving, arrived, turned, gcorr, parts_a, stats_a, sums_a, corr = together(
                (moving, arrived, turned, gcorr, parts_a, stats_a, sums_a, corr)
            )
        elif step == 1:
            sums_a = sums_a[:, :half] + swap(sums_a[:, half:], 1)
            both_g = jnp.sum(gcorr.astype(f32) * corr, axis=1)
            near_block = [swap(jnp.concatenate([gcorr] + turned[0], 0), 1)]
            sibling.append(
                [
                    near_block[0][narrow + s * cuts_g[1] : narrow + (s + 1) * cuts_g[1]]
                    for s in range(cubes - 1)
                ]
            )
            own = jnp.concatenate([gcorr, near_block[0][:narrow]], 1)
            moving, arrived, turned, gcorr, sibling, parts_a, own, stats_a, sums_a, both_g = together(
                (moving, arrived, turned, gcorr, sibling, parts_a, own, stats_a, sums_a, both_g)
            )
        else:
            cross = cross_products(0, norm_b, moving, orders, k)
            grad_nb = dot(near, own, ((1,), (1,)))
            stats_b = jnp.stack([jnp.sum(gcorr.astype(f32) * sums_a[3:4], axis=1), both_g])
            stats_a = stats_a + swap_k(stats_a, 4)
            line_a, line_b = line(sums_a), line(sums_b)
            (
                arrived, turned, sibling, far_0, cross, mean_ah, inv_ah, grad_nb, stats_a, stats_b,
                line_a, line_b,
            ) = together(
                (
                    arrived, turned, sibling, far_0, cross, mean_ah, inv_ah, grad_nb, stats_a,
                    stats_b, line_a, line_b,
                )
            )
        if step < 2:
            moving = double(moving, arrived)

    for step in (1, 2):
        sibling.append([swap(x, 1) for x in turned[step]])
    loss = jnp.broadcast_to(stats_a[2:3, :128], (8, 128))
    first_a = stats_a[0:1] / count
    second_a = line_a[0] * stats_a[1:2] + line_a[1] * first_a
    all_a = jnp.concatenate([parts_a[0][:, :half]] + far_0 + [other_a], 0)
    out_a = cross_products(
        1, norm_b, arrived, orders, k, cross, all_a, mean_ah, inv_ah, first_a, second_a
    )
    out_a, stats_b, sibling, rest, loss = together((out_a, stats_b, sibling, rest, loss))
    for mask in h_masks:
        stats_b = stats_b + swap(stats_b, mask)

    for s in range(1, cubes):
        for side, blocks in enumerate((turned, sibling)):
            block = jnp.concatenate([x[cubes - s - 1] for x in blocks], 0)
            start = (s - 1) * wide + side * half
            grad_nb = grad_nb + dot(rest[:, start : start + half], block, ((1,), (1,)))

    mine = cubes * rows
    both = jnp.concatenate([out_a[:mine], swap(out_a[mine:], 1)], 1)
    both, grad_nb, loss, stats_b = together((both, grad_nb, loss, stats_b))
    stats_b = stats_b + swap(stats_b, 1)
    loss = loss + swap(loss, 1)
    first_b = stats_b[0:1] / count
    second_b = line_b[0] * stats_b[1:2] + line_b[1] * first_b
    for mask in h_masks:
        loss = loss + swap(loss, mask)
    blocks = [both[s * rows : (s + 1) * rows] for s in range(cubes)]
    blocks = [blocks[0]] + [turn(blocks[s], -s) for s in range(1, cubes)]
    grad_a = place(blocks, jnp.stack(at))
    out_b = exchange(finish(grad_nb, near_b, mean_bn, inv_bn, first_b, second_b, k))
    grad_b = jnp.concatenate([out_b[r] for r in range(cube)], 1)
    return (loss[0, 0], grad_a, grad_b)


def solution(mesh):
    return jax.shard_map(
        shards,
        mesh=mesh,
        in_specs=(P("dp", None), P("dp", None)),
        out_specs=(P(), P("dp", None), P("dp", None)),
        check_vma=False,
    )
```

profile of v0, /device:TPU:0, one launch (start us, length us, event | category | flops | bytes accessed | tf_op | source)
XLA Modules:
  0.0 312.1 jit_solution(12157182552004790912)
XLA Ops:
  3.2 2.1 shard_map.49
  8.6 6.2 %all-to-all-start = ((bf16[8,128,512]{2,1,0:T(8,128)(2,1)}), bf16[8,128,512]{2,1,0:T(8,128)(2,1)S(1)}, u32[]{:S(2)}, u32[]{:S(2)}) async-start(bf16[8,128,512]{2,1,0:T(8,128)(2,1)} %get-tuple-element.210), calls=%async_computation | async-start | bytes 2097152 | tf_op jit(solution)/shard_map/all_to_all | solution.py:334
  14.9 2.0 collective-permute-start.2
  19.9 2.7 collective-permute-start.5
  24.7 12.8 %collective-permute-done.4 = f32[4,4096]{1,0:T(4,128)S(1)} collective-permute-done((f32[4,4096]{1,0:T(4,128)S(1)}, f32[4,4096]{1,0:T(4,128)S(1)}, u32[]{:S(2)}, u32[]{:S(2)}) %collective-permute-start.4) | collective-permute-done | bytes 65568 | tf_op jit(solution)/shard_map/ppermute | solution.py:320
  37.5 2.2 collective-permute-done.refs_3_
  42.9 1.8 collective-permute-start.6
  44.7 1.6 collective-permute-start.7
  49.1 4.7 %collective-permute-done.10 = f32[4,4096]{1,0:T(4,128)S(1)} collective-permute-done((f32[4,4096]{1,0:T(4,128)S(1)}, f32[4,4096]{1,0:T(4,128)S(1)}, u32[]{:S(2)}, u32[]{:S(2)}) %collective-permute-start.10) | collective-permute-done | bytes 65568 | tf_op jit(solution)/shard_map/ppermute | solution.py:320
  54.5 3.7 %collective-permute-done.11 = f32[4,4096]{1,0:T(4,128)S(1)} collective-permute-done((f32[4,4096]{1,0:T(4,128)S(1)}, f32[4,4096]{1,0:T(4,128)S(1)}, u32[]{:S(2)}, u32[]{:S(2)}) %collective-permute-start.11) | collective-permute-done | bytes 65568 | tf_op jit(solution)/shard_map/ppermute | solution.py:320
  61.0 3.5 %collective-permute-done.9 = bf16[64,4096]{1,0:T(8,128)(2,1)} collective-permute-done((bf16[64,4096]{1,0:T(8,128)(2,1)S(1)}, bf16[64,4096]{1,0:T(8,128)(2,1)}, u32[]{:S(2)}, u32[]{:S(2)}) %collective-permute-start.9) | collective-permute-done | bytes 524320 | tf_op jit(solution)/shard_map/ppermute | solution.py:326
  69.6 2.1 collective-permute-start.14
  71.7 4.1 %collective-permute-start.15 = (bf16[64,4096]{1,0:T(8,128)(2,1)S(1)}, bf16[64,4096]{1,0:T(8,128)(2,1)S(1)}, u32[]{:S(2)}, u32[]{:S(2)}) collective-permute-start(bf16[64,4096]{1,0:T(8,128)(2,1)S(1)} %copy-done.31), channel_id=1, source_target_pairs={{0,16},{1,17},{2,18},{3,19},{4,20},{5,21},{6,22},{7,23},{8,24},{9,... | collective-permute-start | bytes 1572872 | tf_op jit(solution)/shard_map/ppermute | solution.py:326
  79.4 14.5 %collective-permute-done.14.refs_5_ = bf16[512,512]{1,0:T(8,128)(2,1)S(1)} collective-permute-done((bf16[512,512]{1,0:T(8,128)(2,1)S(1)}, bf16[512,512]{1,0:T(8,128)(2,1)S(1)}, u32[]{:S(2)}, u32[]{:S(2)}) %collective-permute-start.14) | collective-permute-done | bytes 524320 | tf_op jit(solution)/shard_map/ppermute | solution.py:320
  94.0 1.5 shard_map.53
  98.5 3.5 %collective-permute-start.18 = (bf16[128,768]{1,0:T(8,128)(2,1)S(1)}, bf16[128,768]{1,0:T(8,128)(2,1)S(1)}, u32[]{:S(2)}, u32[]{:S(2)}) collective-permute-start(bf16[128,768]{1,0:T(8,128)(2,1)S(1)} %copy-done.14), channel_id=1, source_target_pairs={{0,8},{1,9},{2,10},{3,11},{4,12},{5,13},{6,14},{7,15},{8,0},{9,1},... | collective-permute-start | bytes 589832 | tf_op jit(solution)/shard_map/ppermute | solution.py:320
  105.5 1.8 collective-permute-done.18.refs_3_
  108.7 2.8 collective-permute-start.24
  115.8 4.0 %shard_map.55 = f32[4,2048]{1,0:T(4,128)S(1)} custom-call(f32[1,2048]{1,0:T(1,128)S(1)} %get-tuple-element.410.mean_ref, f32[1,2048]{1,0:T(1,128)S(1)} %get-tuple-element.408.inv_ref, bf16[512,768]{1,0:T(8,128)(2,1)S(1)} %get-tuple-element.262.refs_0_, bf16[512,768]{1,0:T(8,128)(2,1)S(1)} %collective-permute-done.12.refs_1_, ...), custom_call_target="tpu_custom_call" | custom-call | tf_op jit(solution)/shard_map/pallas_call | solution.py:169
  119.8 2.9 collective-permute-done.23.refs_5_
  122.7 5.7 %collective-permute-done.24 = bf16[192,1024]{1,0:T(8,128)(2,1)S(1)} collective-permute-done((bf16[192,1024]{1,0:T(8,128)(2,1)S(1)}, bf16[192,1024]{1,0:T(8,128)(2,1)S(1)}, u32[]{:S(2)}, u32[]{:S(2)}) %collective-permute-start.24) | collective-permute-done | bytes 393248 | tf_op jit(solution)/shard_map/ppermute | solution.py:326
  128.4 1.6 collective-permute-done.22.refs_4_
  130.1 3.0 collective-permute-start.30
  136.4 1.6 multiply_convert_fusion
  138.0 7.7 %collective-permute-done.31 = f32[4,2560]{1,0:T(4,128)S(1)} collective-permute-done((f32[4,2560]{1,0:T(4,128)S(1)}, f32[4,2560]{1,0:T(4,128)S(1)}, u32[]{:S(2)}, u32[]{:S(2)}) %collective-permute-start.31) | collective-permute-done | bytes 40992 | tf_op jit(solution)/shard_map/ppermute | solution.py:326
  145.6 10.0 %collective-permute-done.30 = bf16[256,1024]{1,0:T(8,128)(2,1)S(1)} collective-permute-done((bf16[256,1024]{1,0:T(8,128)(2,1)S(1)}, bf16[256,1024]{1,0:T(8,128)(2,1)S(1)}, u32[]{:S(2)}, u32[]{:S(2)}) %collective-permute-start.30) | collective-permute-done | bytes 524320 | tf_op jit(solution)/shard_map/ppermute | solution.py:326
  155.7 1.5 shard_map.57
  160.5 1.6 collective-permute-start.33
  163.4 2.3 pad_maximum_fusion.rows_ref
  166.1 3.4 %collective-permute-done.33 = bf16[64,1024]{1,0:T(8,128)(2,1)S(1)} collective-permute-done((bf16[64,1024]{1,0:T(8,128)(2,1)S(1)}, bf16[64,1024]{1,0:T(8,128)(2,1)S(1)}, u32[]{:S(2)}, u32[]{:S(2)}) %collective-permute-start.33) | collective-permute-done | bytes 131104 | tf_op jit(solution)/shard_map/ppermute | solution.py:326
  169.9 2.6 fusion.6
  176.2 2.4 collective-permute-start.36
  178.7 4.0 %shard_map.58 = f32[4,2048]{1,0:T(4,128)S(1)} custom-call(f32[1,2048]{1,0:T(1,128)S(1)} %get-tuple-element.411.mean_ref, f32[1,2048]{1,0:T(1,128)S(1)} %get-tuple-element.409.inv_ref, bf16[512,768]{1,0:T(8,128)(2,1)S(1)} %get-tuple-element.304.refs_0_, bf16[512,768]{1,0:T(8,128)(2,1)S(1)} %collective-permute-done.27.refs_1_, ...), custom_call_target="tpu_custom_call" | custom-call | tf_op jit(solution)/shard_map/pallas_call | solution.py:169
  184.2 2.3 collective-permute-done.41
  186.6 7.8 %collective-permute-done.39 = bf16[192,1024]{1,0:T(8,128)(2,1)S(1)} collective-permute-done((bf16[192,1024]{1,0:T(8,128)(2,1)S(1)}, bf16[192,1024]{1,0:T(8,128)(2,1)S(1)}, u32[]{:S(2)}, u32[]{:S(2)}) %collective-permute-start.39) | collective-permute-done | bytes 393248 | tf_op jit(solution)/shard_map/ppermute | solution.py:326
  199.0 2.4 collective-permute-start.45
  202.5 20.4 %collective-permute-done.45 = bf16[192,1024]{1,0:T(8,128)(2,1)S(1)} collective-permute-done((bf16[192,1024]{1,0:T(8,128)(2,1)S(1)}, bf16[192,1024]{1,0:T(8,128)(2,1)S(1)}, u32[]{:S(2)}, u32[]{:S(2)}) %collective-permute-start.45) | collective-permute-done | bytes 393248 | tf_op jit(solution)/shard_map/ppermute | solution.py:326
  222.9 2.2 collective-permute-done.43.refs_4_
  228.7 3.7 %fusion.63 = f32[1024,512]{1,0:T(8,128)} fusion(bf16[1024,2048]{1,0:T(8,128)(2,1)S(1)} %shard_map.57, bf16[512,2048]{1,0:T(8,128)(2,1)S(1)} %pad_maximum_fusion.1), kind=kOutput, calls=%fused_computation.126 | convolution fusion | flops 2147483648 | bytes 8388608 | tf_op jit(solution)/shard_map/dot_general | solution.py:250
  232.5 1.8 collective-permute-start.51
  235.4 6.6 %shard_map.61.refs_0_ = f32[512,1024]{1,0:T(8,128)} custom-call(s32[1]{0:T(128)} %bitcast.k_ref, bf16[512,4096]{1,0:T(8,128)(2,1)} %pad_maximum_fusion.rows_ref, bf16[2048,384]{1,0:T(8,128)(2,1)S(1)} %get-tuple-element.332.refs_0_, bf16[2048,384]{1,0:T(8,128)(2,1)S(1)} %get-tuple-element.333.refs_1_, bf16[2048,256]{1,0:T(8,128)(2,1)S(1)} %get-tuple-element.334.refs_2_), custom_call_target="tpu_custom_call" | custom-call | flops 2147483648 | bytes 8388608 | tf_op jit(solution)/shard_map/pallas_call | solution.py:293
  242.0 20.0 %collective-permute-done.52 = f32[3,1024]{1,0:T(4,128)S(1)} collective-permute-done((f32[3,1024]{1,0:T(4,128)S(1)}, f32[3,1024]{1,0:T(4,128)S(1)}, u32[]{:S(2)}, u32[]{:S(2)}) %collective-permute-start.52) | collective-permute-done | bytes 12320 | tf_op jit(solution)/shard_map/ppermute | solution.py:320
  264.6 6.3 %shard_map.62 = bf16[512,1024]{1,0:T(8,128)(2,1)S(1)} custom-call(s32[1]{0:T(128)} %bitcast.k_ref, bf16[512,4096]{1,0:T(8,128)(2,1)} %pad_maximum_fusion.rows_ref, f32[512,1024]{1,0:T(8,128)} %shard_map.61.refs_0_, bf16[512,1024]{1,0:T(8,128)(2,1)S(1)} %pad_maximum_fusion.3.refs_1_, f32[1,1024]{1,0:T(1,128)S(1)} %slice.246.refs_2_, ...), custom_call_target="tpu_custom_call" | custom-call | flops 2147483648 | bytes 8388608 | tf_op jit(solution)/shard_map/pallas_call | solution.py:293
  277.0 1.7 shard_map.64
  278.8 3.6 %all-to-all-start.1 = ((bf16[8,128,512]{2,1,0:T(8,128)(2,1)}), bf16[8,128,512]{2,1,0:T(8,128)(2,1)S(1)}, u32[]{:S(2)}, u32[]{:S(2)}) async-start(bf16[8,128,512]{2,1,0:T(8,128)(2,1)} %shard_map.64), calls=%async_computation.1 | async-start | bytes 2097152 | tf_op jit(solution)/shard_map/all_to_all | solution.py:334
  285.1 1.5 collective-permute-start.58
  286.6 22.3 %collective-permute-done.58 = f32[8,128]{1,0:T(8,128)S(1)} collective-permute-done((f32[8,128]{1,0:T(8,128)S(1)}, f32[8,128]{1,0:T(8,128)S(1)}, u32[]{:S(2)}, u32[]{:S(2)}) %collective-permute-start.58) | collective-permute-done | bytes 4128 | tf_op jit(solution)/shard_map/ppermute | solution.py:320
  309.4 1.6 shard_map.63
  (273 shorter events, 78.7 us)
Async XLA Ops:
  8.6 55.9 %all-to-all-start = ((bf16[8,128,512]{2,1,0:T(8,128)(2,1)}), bf16[8,128,512]{2,1,0:T(8,128)(2,1)S(1)}, u32[]{:S(2)}, u32[]{:S(2)}) async-start(bf16[8,128,512]{2,1,0:T(8,128)(2,1)} %get-tuple-element.210), calls=%async_computation | async-start | bytes 2097152 | tf_op jit(solution)/shard_map/all_to_all | solution.py:334
  14.8 7.7 %collective-permute-start.3 = (f32[4,4096]{1,0:T(4,128)}, f32[4,4096]{1,0:T(4,128)S(1)}, u32[]{:S(2)}, u32[]{:S(2)}) collective-permute-start(f32[4,4096]{1,0:T(4,128)} %copy-done.25), channel_id=1, source_target_pairs={{0,1},{1,0},{2,3},{3,2},{4,5},{5,4},{6,7},{7,6},{8,9},{9,8},{10,11... | collective-permute-start | bytes 196616 | tf_op jit(solution)/shard_map/ppermute | solution.py:320
  14.9 22.6 %collective-permute-start.2 = (bf16[128,512]{1,0:T(8,128)(2,1)}, bf16[128,512]{1,0:T(8,128)(2,1)S(1)}, u32[]{:S(2)}, u32[]{:S(2)}) collective-permute-start(bf16[128,512]{1,0:T(8,128)(2,1)} %copy-done.23), channel_id=1, source_target_pairs={{0,4},{1,5},{2,6},{3,7},{4,0},{5,1},{6,2},{7,3},{8,12},{9,13},{10,... | collective-permute-start | bytes 393224 | tf_op jit(solution)/shard_map/ppermute | solution.py:320
  16.9 22.8 %collective-permute-start = (bf16[128,768]{1,0:T(8,128)(2,1)S(1)}, bf16[128,768]{1,0:T(8,128)(2,1)S(1)}, u32[]{:S(2)}, u32[]{:S(2)}) collective-permute-start(bf16[128,768]{1,0:T(8,128)(2,1)S(1)} %get-tuple-element.198.refs_0_), channel_id=1, source_target_pairs={{0,8},{1,9},{2,10},{3,11},{4,12},{5,13},{6,14},{7,15},{8,0},{9,1},... | collective-permute-start | bytes 589832 | tf_op jit(solution)/shard_map/ppermute | solution.py:320
  18.4 21.3 %collective-permute-start.1 = (bf16[128,768]{1,0:T(8,128)(2,1)S(1)}, bf16[128,768]{1,0:T(8,128)(2,1)S(1)}, u32[]{:S(2)}, u32[]{:S(2)}) collective-permute-start(bf16[128,768]{1,0:T(8,128)(2,1)S(1)} %get-tuple-element.199.refs_1_), channel_id=1, source_target_pairs={{0,2},{1,3},{2,0},{3,1},{4,6},{5,7},{6,4},{7,5},{8,10},{9,11},{10,... | collective-permute-start | bytes 589832 | tf_op jit(solution)/shard_map/ppermute | solution.py:320
  19.9 19.8 %collective-permute-start.5 = (bf16[128,1024]{1,0:T(8,128)(2,1)S(1)}, bf16[128,1024]{1,0:T(8,128)(2,1)S(1)}, u32[]{:S(2)}, u32[]{:S(2)}) collective-permute-start(bf16[128,1024]{1,0:T(8,128)(2,1)S(1)} %slice.213), channel_id=1, source_target_pairs={{0,16},{1,17},{2,18},{3,19},{4,20},{5,21},{6,22},{7,23},{8,24},{9,... | collective-permute-start | bytes 786440 | tf_op jit(solution)/shard_map/ppermute | solution.py:326
  23.4 14.1 %collective-permute-start.4 = (f32[4,4096]{1,0:T(4,128)S(1)}, f32[4,4096]{1,0:T(4,128)S(1)}, u32[]{:S(2)}, u32[]{:S(2)}) collective-permute-start(f32[4,4096]{1,0:T(4,128)S(1)} %add.161), channel_id=1, source_target_pairs={{0,16},{1,17},{2,18},{3,19},{4,20},{5,21},{6,22},{7,23},{8,24},{9,... | collective-permute-start | bytes 196616 | tf_op jit(solution)/shard_map/ppermute | solution.py:320
  39.7 24.8 %collective-permute-start.9 = (bf16[64,4096]{1,0:T(8,128)(2,1)S(1)}, bf16[64,4096]{1,0:T(8,128)(2,1)}, u32[]{:S(2)}, u32[]{:S(2)}) collective-permute-start(bf16[64,4096]{1,0:T(8,128)(2,1)S(1)} %get-tuple-element.207), channel_id=1, source_target_pairs={{0,16},{1,17},{2,18},{3,19},{4,20},{5,21},{6,22},{7,23},{8,24},{9,... | collective-permute-start | bytes 1572872 | tf_op jit(solution)/shard_map/ppermute | solution.py:326
  42.9 16.6 %collective-permute-start.6 = (bf16[256,768]{1,0:T(8,128)(2,1)S(1)}, bf16[256,768]{1,0:T(8,128)(2,1)S(1)}, u32[]{:S(2)}, u32[]{:S(2)}) collective-permute-start(bf16[256,768]{1,0:T(8,128)(2,1)S(1)} %get-tuple-element.214.refs_0_), channel_id=1, source_target_pairs={{0,4},{1,5},{2,6},{3,7},{4,0},{5,1},{6,2},{7,3},{8,12},{9,13},{10,... | collective-permute-start | bytes 1179656 | tf_op jit(solution)/shard_map/ppermute | solution.py:320
  44.7 15.5 %collective-permute-start.7 = (bf16[256,768]{1,0:T(8,128)(2,1)S(1)}, bf16[256,768]{1,0:T(8,128)(2,1)S(1)}, u32[]{:S(2)}, u32[]{:S(2)}) collective-permute-start(bf16[256,768]{1,0:T(8,128)(2,1)S(1)} %get-tuple-element.215.refs_1_), channel_id=1, source_target_pairs={{0,8},{1,9},{2,10},{3,11},{4,12},{5,13},{6,14},{7,15},{8,0},{9,1},... | collective-permute-start | bytes 1179656 | tf_op jit(solution)/shard_map/ppermute | solution.py:320
  46.4 12.4 %collective-permute-start.8 = (bf16[256,512]{1,0:T(8,128)(2,1)S(1)}, bf16[256,512]{1,0:T(8,128)(2,1)S(1)}, u32[]{:S(2)}, u32[]{:S(2)}) collective-permute-start(bf16[256,512]{1,0:T(8,128)(2,1)S(1)} %get-tuple-element.216.refs_2_), channel_id=1, source_target_pairs={{0,2},{1,3},{2,0},{3,1},{4,6},{5,7},{6,4},{7,5},{8,10},{9,11},{10,... | collective-permute-start | bytes 786440 | tf_op jit(solution)/shard_map/ppermute | solution.py:320
  64.5 13.3 %collective-permute-start.16 = (f32[4,4096]{1,0:T(4,128)}, f32[4,4096]{1,0:T(4,128)}, u32[]{:S(2)}, u32[]{:S(2)}) collective-permute-start(f32[4,4096]{1,0:T(4,128)} %add.164), channel_id=1, source_target_pairs={{0,8},{1,9},{2,10},{3,11},{4,12},{5,13},{6,14},{7,15},{8,0},{9,1},... | collective-permute-start | bytes 196616 | tf_op jit(solution)/shard_map/ppermute | solution.py:320
  69.6 24.4 %collective-permute-start.14 = (bf16[512,512]{1,0:T(8,128)(2,1)S(1)}, bf16[512,512]{1,0:T(8,128)(2,1)S(1)}, u32[]{:S(2)}, u32[]{:S(2)}) collective-permute-start(bf16[512,512]{1,0:T(8,128)(2,1)S(1)} %get-tuple-element.266.refs_4_), channel_id=1, source_target_pairs={{0,8},{1,9},{2,10},{3,11},{4,12},{5,13},{6,14},{7,15},{8,0},{9,1},... | collective-permute-start | bytes 1572872 | tf_op jit(solution)/shard_map/ppermute | solution.py:320
  71.7 22.3 %collective-permute-start.15 = (bf16[64,4096]{1,0:T(8,128)(2,1)S(1)}, bf16[64,4096]{1,0:T(8,128)(2,1)S(1)}, u32[]{:S(2)}, u32[]{:S(2)}) collective-permute-start(bf16[64,4096]{1,0:T(8,128)(2,1)S(1)} %copy-done.31), channel_id=1, source_target_pairs={{0,16},{1,17},{2,18},{3,19},{4,20},{5,21},{6,22},{7,23},{8,24},{9,... | collective-permute-start | bytes 1572872 | tf_op jit(solution)/shard_map/ppermute | solution.py:326
  75.8 18.2 %collective-permute-start.12 = (bf16[512,768]{1,0:T(8,128)(2,1)S(1)}, bf16[512,768]{1,0:T(8,128)(2,1)S(1)}, u32[]{:S(2)}, u32[]{:S(2)}) collective-permute-start(bf16[512,768]{1,0:T(8,128)(2,1)S(1)} %get-tuple-element.262.refs_0_), channel_id=1, source_target_pairs={{0,2},{1,3},{2,0},{3,1},{4,6},{5,7},{6,4},{7,5},{8,10},{9,11},{10,... | collective-permute-start | bytes 2359304 | tf_op jit(solution)/shard_map/ppermute | solution.py:320
  77.3 16.7 %collective-permute-start.13 = (bf16[512,768]{1,0:T(8,128)(2,1)S(1)}, bf16[512,768]{1,0:T(8,128)(2,1)S(1)}, u32[]{:S(2)}, u32[]{:S(2)}) collective-permute-start(bf16[512,768]{1,0:T(8,128)(2,1)S(1)} %get-tuple-element.264.refs_2_), channel_id=1, source_target_pairs={{0,4},{1,5},{2,6},{3,7},{4,0},{5,1},{6,2},{7,3},{8,12},{9,13},{10,... | collective-permute-start | bytes 2359304 | tf_op jit(solution)/shard_map/ppermute | solution.py:320
  96.9 8.0 %collective-permute-start.17 = (f32[512,1024]{1,0:T(8,128)S(1)}, f32[512,1024]{1,0:T(8,128)S(1)}, u32[]{:S(2)}, u32[]{:S(2)}) collective-permute-start(f32[512,1024]{1,0:T(8,128)S(1)} %fusion.13), channel_id=1, source_target_pairs={{0,1},{1,0},{2,3},{3,2},{4,5},{5,4},{6,7},{7,6},{8,9},{9,8},{10,11... | collective-permute-start | bytes 6291464 | tf_op jit(solution)/shard_map/ppermute | solution.py:320
  97.0 8.4 %collective-permute-start.20 = (bf16[128,512]{1,0:T(8,128)(2,1)S(1)}, bf16[128,512]{1,0:T(8,128)(2,1)S(1)}, u32[]{:S(2)}, u32[]{:S(2)}) collective-permute-start(bf16[128,512]{1,0:T(8,128)(2,1)S(1)} %copy-done.22), channel_id=1, source_target_pairs={{0,4},{1,5},{2,6},{3,7},{4,0},{5,1},{6,2},{7,3},{8,12},{9,13},{10,... | collective-permute-start | bytes 393224 | tf_op jit(solution)/shard_map/ppermute | solution.py:320
  98.5 8.7 %collective-permute-start.18 = (bf16[128,768]{1,0:T(8,128)(2,1)S(1)}, bf16[128,768]{1,0:T(8,128)(2,1)S(1)}, u32[]{:S(2)}, u32[]{:S(2)}) collective-permute-start(bf16[128,768]{1,0:T(8,128)(2,1)S(1)} %copy-done.14), channel_id=1, source_target_pairs={{0,8},{1,9},{2,10},{3,11},{4,12},{5,13},{6,14},{7,15},{8,0},{9,1},... | collective-permute-start | bytes 589832 | tf_op jit(solution)/shard_map/ppermute | solution.py:320
  103.5 16.3 %collective-permute-start.25 = (bf16[256,1024]{1,0:T(8,128)(2,1)S(1)}, bf16[256,1024]{1,0:T(8,128)(2,1)S(1)}, u32[]{:S(2)}, u32[]{:S(2)}) collective-permute-start(bf16[256,1024]{1,0:T(8,128)(2,1)S(1)} %pad_maximum_fusion.5), channel_id=1, source_target_pairs={{0,1},{1,0},{2,3},{3,2},{4,5},{5,4},{6,7},{7,6},{8,9},{9,8},{10,11... | collective-permute-start | bytes 1572872 | tf_op jit(solution)/shard_map/ppermute | solution.py:320
  108.7 19.6 %collective-permute-start.24 = (bf16[192,1024]{1,0:T(8,128)(2,1)S(1)}, bf16[192,1024]{1,0:T(8,128)(2,1)S(1)}, u32[]{:S(2)}, u32[]{:S(2)}) collective-permute-start(bf16[192,1024]{1,0:T(8,128)(2,1)S(1)} %slice.224), channel_id=1, source_target_pairs={{0,16},{1,17},{2,18},{3,19},{4,20},{5,21},{6,22},{7,23},{8,24},{9,... | collective-permute-start | bytes 1179656 | tf_op jit(solution)/shard_map/ppermute | solution.py:326
  111.6 16.8 %collective-permute-start.21 = (bf16[256,768]{1,0:T(8,128)(2,1)S(1)}, bf16[256,768]{1,0:T(8,128)(2,1)S(1)}, u32[]{:S(2)}, u32[]{:S(2)}) collective-permute-start(bf16[256,768]{1,0:T(8,128)(2,1)S(1)} %get-tuple-element.269.refs_0_), channel_id=1, source_target_pairs={{0,4},{1,5},{2,6},{3,7},{4,0},{5,1},{6,2},{7,3},{8,12},{9,13},{10,... | collective-permute-start | bytes 1179656 | tf_op jit(solution)/shard_map/ppermute | solution.py:320
  112.3 17.7 %collective-permute-start.22 = (bf16[256,768]{1,0:T(8,128)(2,1)S(1)}, bf16[256,768]{1,0:T(8,128)(2,1)S(1)}, u32[]{:S(2)}, u32[]{:S(2)}) collective-permute-start(bf16[256,768]{1,0:T(8,128)(2,1)S(1)} %get-tuple-element.270.refs_1_), channel_id=1, source_target_pairs={{0,8},{1,9},{2,10},{3,11},{4,12},{5,13},{6,14},{7,15},{8,0},{9,1},... | collective-permute-start | bytes 1179656 | tf_op jit(solution)/shard_map/ppermute | solution.py:320
  114.3 8.4 %collective-permute-start.23 = (bf16[256,512]{1,0:T(8,128)(2,1)S(1)}, bf16[256,512]{1,0:T(8,128)(2,1)S(1)}, u32[]{:S(2)}, u32[]{:S(2)}) collective-permute-start(bf16[256,512]{1,0:T(8,128)(2,1)S(1)} %get-tuple-element.271.refs_2_), channel_id=1, source_target_pairs={{0,2},{1,3},{2,0},{3,1},{4,6},{5,7},{6,4},{7,5},{8,10},{9,11},{10,... | collective-permute-start | bytes 786440 | tf_op jit(solution)/shard_map/ppermute | solution.py:320
  130.0 15.6 %collective-permute-start.31 = (f32[4,2560]{1,0:T(4,128)S(1)}, f32[4,2560]{1,0:T(4,128)S(1)}, u32[]{:S(2)}, u32[]{:S(2)}) collective-permute-start(f32[4,2560]{1,0:T(4,128)S(1)} %pad_maximum_fusion.7), channel_id=1, source_target_pairs={{0,16},{1,17},{2,18},{3,19},{4,20},{5,21},{6,22},{7,23},{8,24},{9,... | collective-permute-start | bytes 122888 | tf_op jit(solution)/shard_map/ppermute | solution.py:326
  130.1 25.4 %collective-permute-start.30 = (bf16[256,1024]{1,0:T(8,128)(2,1)S(1)}, bf16[256,1024]{1,0:T(8,128)(2,1)S(1)}, u32[]{:S(2)}, u32[]{:S(2)}) collective-permute-start(bf16[256,1024]{1,0:T(8,128)(2,1)S(1)} %slice.226), channel_id=1, source_target_pairs={{0,16},{1,17},{2,18},{3,19},{4,20},{5,21},{6,22},{7,23},{8,24},{9,... | collective-permute-start | bytes 1572872 | tf_op jit(solution)/shard_map/ppermute | solution.py:326
  133.3 22.3 %collective-permute-start.29 = (bf16[512,512]{1,0:T(8,128)(2,1)S(1)}, bf16[512,512]{1,0:T(8,128)(2,1)S(1)}, u32[]{:S(2)}, u32[]{:S(2)}) collective-permute-start(bf16[512,512]{1,0:T(8,128)(2,1)S(1)} %get-tuple-element.308.refs_4_), channel_id=1, source_target_pairs={{0,8},{1,9},{2,10},{3,11},{4,12},{5,13},{6,14},{7,15},{8,0},{9,1},... | collective-permute-start | bytes 1572872 | tf_op jit(solution)/shard_map/ppermute | solution.py:320
  133.4 22.2 %collective-permute-start.27 = (bf16[512,768]{1,0:T(8,128)(2,1)S(1)}, bf16[512,768]{1,0:T(8,128)(2,1)S(1)}, u32[]{:S(2)}, u32[]{:S(2)}) collective-permute-start(bf16[512,768]{1,0:T(8,128)(2,1)S(1)} %get-tuple-element.304.refs_0_), channel_id=1, source_target_pairs={{0,2},{1,3},{2,0},{3,1},{4,6},{5,7},{6,4},{7,5},{8,10},{9,11},{10,... | collective-permute-start | bytes 2359304 | tf_op jit(solution)/shard_map/ppermute | solution.py:320
  134.9 20.7 %collective-permute-start.28 = (bf16[512,768]{1,0:T(8,128)(2,1)S(1)}, bf16[512,768]{1,0:T(8,128)(2,1)S(1)}, u32[]{:S(2)}, u32[]{:S(2)}) collective-permute-start(bf16[512,768]{1,0:T(8,128)(2,1)S(1)} %get-tuple-element.306.refs_2_), channel_id=1, source_target_pairs={{0,4},{1,5},{2,6},{3,7},{4,0},{5,1},{6,2},{7,3},{8,12},{9,13},{10,... | collective-permute-start | bytes 2359304 | tf_op jit(solution)/shard_map/ppermute | solution.py:320
  155.6 7.8 %collective-permute-start.35 = (bf16[256,4096]{1,0:T(8,128)(2,1)S(1)}, bf16[256,4096]{1,0:T(8,128)(2,1)S(1)}, u32[]{:S(2)}, u32[]{:S(2)}) collective-permute-start(bf16[256,4096]{1,0:T(8,128)(2,1)S(1)} %multiply_convert_fusion), channel_id=1, source_target_pairs={{0,1},{1,0},{2,3},{3,2},{4,5},{5,4},{6,7},{7,6},{8,9},{9,8},{10,11... | collective-permute-start | bytes 6291464 | tf_op jit(solution)/shard_map/ppermute | solution.py:320
  160.5 9.0 %collective-permute-start.33 = (bf16[64,1024]{1,0:T(8,128)(2,1)S(1)}, bf16[64,1024]{1,0:T(8,128)(2,1)S(1)}, u32[]{:S(2)}, u32[]{:S(2)}) collective-permute-start(bf16[64,1024]{1,0:T(8,128)(2,1)S(1)} %slice.229), channel_id=1, source_target_pairs={{0,16},{1,17},{2,18},{3,19},{4,20},{5,21},{6,22},{7,23},{8,24},{9,... | collective-permute-start | bytes 393224 | tf_op jit(solution)/shard_map/ppermute | solution.py:326
  173.4 9.3 %collective-permute-start.40 = (f32[3,1024]{1,0:T(4,128)S(1)}, f32[3,1024]{1,0:T(4,128)S(1)}, u32[]{:S(2)}, u32[]{:S(2)}) collective-permute-start(f32[3,1024]{1,0:T(4,128)S(1)} %maximum_maximum_fusion), channel_id=1, source_target_pairs={{0,2},{1,3},{2,0},{3,1},{4,6},{5,7},{6,4},{7,5},{8,10},{9,11},{10,... | collective-permute-start | bytes 36872 | tf_op jit(solution)/shard_map/ppermute | solution.py:320
  175.0 11.6 %collective-permute-start.38 = (bf16[512,256]{1,0:T(8,128)(2,1)S(1)}, bf16[512,256]{1,0:T(8,128)(2,1)S(1)}, u32[]{:S(2)}, u32[]{:S(2)}) collective-permute-start(bf16[512,256]{1,0:T(8,128)(2,1)S(1)} %slice.286.refs_2_), channel_id=1, source_target_pairs={{0,4},{1,5},{2,6},{3,7},{4,0},{5,1},{6,2},{7,3},{8,12},{9,13},{10,... | collective-permute-start | bytes 786440 | tf_op jit(solution)/shard_map/ppermute | solution.py:320
  175.6 18.7 %collective-permute-start.39 = (bf16[192,1024]{1,0:T(8,128)(2,1)S(1)}, bf16[192,1024]{1,0:T(8,128)(2,1)S(1)}, u32[]{:S(2)}, u32[]{:S(2)}) collective-permute-start(bf16[192,1024]{1,0:T(8,128)(2,1)S(1)} %slice.287), channel_id=1, source_target_pairs={{0,16},{1,17},{2,18},{3,19},{4,20},{5,21},{6,22},{7,23},{8,24},{9,... | collective-permute-start | bytes 1179656 | tf_op jit(solution)/shard_map/ppermute | solution.py:326
  175.6 18.7 %collective-permute-start.37 = (bf16[512,384]{1,0:T(8,128)(2,1)S(1)}, bf16[512,384]{1,0:T(8,128)(2,1)S(1)}, u32[]{:S(2)}, u32[]{:S(2)}) collective-permute-start(bf16[512,384]{1,0:T(8,128)(2,1)S(1)} %get-tuple-element.311.refs_1_), channel_id=1, source_target_pairs={{0,2},{1,3},{2,0},{3,1},{4,6},{5,7},{6,4},{7,5},{8,10},{9,11},{10,... | collective-permute-start | bytes 1179656 | tf_op jit(solution)/shard_map/ppermute | solution.py:320
  176.2 18.6 %collective-permute-start.36 = (bf16[512,384]{1,0:T(8,128)(2,1)S(1)}, bf16[512,384]{1,0:T(8,128)(2,1)S(1)}, u32[]{:S(2)}, u32[]{:S(2)}) collective-permute-start(bf16[512,384]{1,0:T(8,128)(2,1)S(1)} %get-tuple-element.310.refs_0_), channel_id=1, source_target_pairs={{0,8},{1,9},{2,10},{3,11},{4,12},{5,13},{6,14},{7,15},{8,0},{9,1},... | collective-permute-start | bytes 1179656 | tf_op jit(solution)/shard_map/ppermute | solution.py:320
  195.5 27.4 %collective-permute-start.42 = (bf16[1024,384]{1,0:T(8,128)(2,1)S(1)}, bf16[1024,384]{1,0:T(8,128)(2,1)S(1)}, u32[]{:S(2)}, u32[]{:S(2)}) collective-permute-start(bf16[1024,384]{1,0:T(8,128)(2,1)S(1)} %get-tuple-element.326.refs_0_), channel_id=1, source_target_pairs={{0,4},{1,5},{2,6},{3,7},{4,0},{5,1},{6,2},{7,3},{8,12},{9,13},{10,... | collective-permute-start | bytes 2359304 | tf_op jit(solution)/shard_map/ppermute | solution.py:320
  197.0 28.1 %collective-permute-start.43 = (bf16[1024,384]{1,0:T(8,128)(2,1)S(1)}, bf16[1024,384]{1,0:T(8,128)(2,1)S(1)}, u32[]{:S(2)}, u32[]{:S(2)}) collective-permute-start(bf16[1024,384]{1,0:T(8,128)(2,1)S(1)} %get-tuple-element.327.refs_1_), channel_id=1, source_target_pairs={{0,8},{1,9},{2,10},{3,11},{4,12},{5,13},{6,14},{7,15},{8,0},{9,1},... | collective-permute-start | bytes 2359304 | tf_op jit(solution)/shard_map/ppermute | solution.py:320
  197.3 25.6 %collective-permute-start.44 = (bf16[1024,256]{1,0:T(8,128)(2,1)S(1)}, bf16[1024,256]{1,0:T(8,128)(2,1)S(1)}, u32[]{:S(2)}, u32[]{:S(2)}) collective-permute-start(bf16[1024,256]{1,0:T(8,128)(2,1)S(1)} %get-tuple-element.328.refs_2_), channel_id=1, source_target_pairs={{0,2},{1,3},{2,0},{3,1},{4,6},{5,7},{6,4},{7,5},{8,10},{9,11},{10,... | collective-permute-start | bytes 1572872 | tf_op jit(solution)/shard_map/ppermute | solution.py:320
  199.0 23.9 %collective-permute-start.45 = (bf16[192,1024]{1,0:T(8,128)(2,1)S(1)}, bf16[192,1024]{1,0:T(8,128)(2,1)S(1)}, u32[]{:S(2)}, u32[]{:S(2)}) collective-permute-start(bf16[192,1024]{1,0:T(8,128)(2,1)S(1)} %slice.237), channel_id=1, source_target_pairs={{0,16},{1,17},{2,18},{3,19},{4,20},{5,21},{6,22},{7,23},{8,24},{9,... | collective-permute-start | bytes 1179656 | tf_op jit(solution)/shard_map/ppermute | solution.py:326
  225.9 36.2 %collective-permute-start.50 = (bf16[2048,256]{1,0:T(8,128)(2,1)S(1)}, bf16[2048,256]{1,0:T(8,128)(2,1)S(1)}, u32[]{:S(2)}, u32[]{:S(2)}) collective-permute-start(bf16[2048,256]{1,0:T(8,128)(2,1)S(1)} %get-tuple-element.334.refs_2_), channel_id=1, source_target_pairs={{0,8},{1,9},{2,10},{3,11},{4,12},{5,13},{6,14},{7,15},{8,0},{9,1},... | collective-permute-start | bytes 3145736 | tf_op jit(solution)/shard_map/ppermute | solution.py:320
  226.8 35.7 %collective-permute-start.48 = (bf16[2048,384]{1,0:T(8,128)(2,1)S(1)}, bf16[2048,384]{1,0:T(8,128)(2,1)S(1)}, u32[]{:S(2)}, u32[]{:S(2)}) collective-permute-start(bf16[2048,384]{1,0:T(8,128)(2,1)S(1)} %get-tuple-element.332.refs_0_), channel_id=1, source_target_pairs={{0,2},{1,3},{2,0},{3,1},{4,6},{5,7},{6,4},{7,5},{8,10},{9,11},{10,... | collective-permute-start | bytes 4718600 | tf_op jit(solution)/shard_map/ppermute | solution.py:320
  228.1 35.4 %collective-permute-start.49 = (bf16[2048,384]{1,0:T(8,128)(2,1)S(1)}, bf16[2048,384]{1,0:T(8,128)(2,1)S(1)}, u32[]{:S(2)}, u32[]{:S(2)}) collective-permute-start(bf16[2048,384]{1,0:T(8,128)(2,1)S(1)} %get-tuple-element.333.refs_1_), channel_id=1, source_target_pairs={{0,4},{1,5},{2,6},{3,7},{4,0},{5,1},{6,2},{7,3},{8,12},{9,13},{10,... | collective-permute-start | bytes 4718600 | tf_op jit(solution)/shard_map/ppermute | solution.py:320
  232.5 29.6 %collective-permute-start.51 = (bf16[256,1024]{1,0:T(8,128)(2,1)S(1)}, bf16[256,1024]{1,0:T(8,128)(2,1)S(1)}, u32[]{:S(2)}, u32[]{:S(2)}) collective-permute-start(bf16[256,1024]{1,0:T(8,128)(2,1)S(1)} %pad_maximum_fusion.6), channel_id=1, source_target_pairs={{0,16},{1,17},{2,18},{3,19},{4,20},{5,21},{6,22},{7,23},{8,24},{9,... | collective-permute-start | bytes 1572872 | tf_op jit(solution)/shard_map/ppermute | solution.py:326
  234.3 27.7 %collective-permute-start.52 = (f32[3,1024]{1,0:T(4,128)S(1)}, f32[3,1024]{1,0:T(4,128)S(1)}, u32[]{:S(2)}, u32[]{:S(2)}) collective-permute-start(f32[3,1024]{1,0:T(4,128)S(1)} %fusion.70), channel_id=1, source_target_pairs={{0,8},{1,9},{2,10},{3,11},{4,12},{5,13},{6,14},{7,15},{8,0},{9,1},... | collective-permute-start | bytes 36872 | tf_op jit(solution)/shard_map/ppermute | solution.py:320
  278.8 32.2 %all-to-all-start.1 = ((bf16[8,128,512]{2,1,0:T(8,128)(2,1)}), bf16[8,128,512]{2,1,0:T(8,128)(2,1)S(1)}, u32[]{:S(2)}, u32[]{:S(2)}) async-start(bf16[8,128,512]{2,1,0:T(8,128)(2,1)} %shard_map.64), calls=%async_computation.1 | async-start | bytes 2097152 | tf_op jit(solution)/shard_map/all_to_all | solution.py:334
  282.4 26.9 %collective-permute-start.59 = (bf16[128,2048]{1,0:T(8,128)(2,1)S(1)}, bf16[128,2048]{1,0:T(8,128)(2,1)S(1)}, u32[]{:S(2)}, u32[]{:S(2)}) collective-permute-start(bf16[128,2048]{1,0:T(8,128)(2,1)S(1)} %get-tuple-element.391), channel_id=1, source_target_pairs={{0,16},{1,17},{2,18},{3,19},{4,20},{5,21},{6,22},{7,23},{8,24},{9,... | collective-permute-start | bytes 1572872 | tf_op jit(solution)/shard_map/ppermute | solution.py:326
  285.1 23.8 %collective-permute-start.58 = (f32[8,128]{1,0:T(8,128)S(1)}, f32[8,128]{1,0:T(8,128)S(1)}, u32[]{:S(2)}, u32[]{:S(2)}) collective-permute-start(f32[8,128]{1,0:T(8,128)S(1)} %add.193), channel_id=1, source_target_pairs={{0,16},{1,17},{2,18},{3,19},{4,20},{5,21},{6,22},{7,23},{8,24},{9,... | collective-permute-start | bytes 12296 | tf_op jit(solution)/shard_map/ppermute | solution.py:320
  (60 other events, 305.5 us)
where the time goes:
time: 313 us; the launch traced here: 312 us
  waiting for transfers between devices  156 us (50%)
  starting transfers between devices  77.5 us (25%)
  Pallas kernels  31.7 us (10%)
  local copies, waits for them, and re-layouts  21 us (7%)
  other arithmetic  12.5 us (4%)
  matrix products  11.4 us (4%)
    ppermute x49, waiting for transfers between devices, swap(): return lax.ppermute(x, 'dp', [(i, i ^ mask) for i in range(devices)])  98.1 us
    ppermute x12, waiting for transfers between devices, turn(): lax.ppermute(x, 'dp', [(i, (i + 2 * cube * step) % devices) for i in rang...  58.4 us
    ppermute x49, starting transfers between devices, swap(): return lax.ppermute(x, 'dp', [(i, i ^ mask) for i in range(devices)])  45.4 us
    ppermute x12, starting transfers between devices, turn(): lax.ppermute(x, 'dp', [(i, (i + 2 * cube * step) % devices) for i in rang...  22.4 us
    unnamed x95, local copies, waits for them, and re-layouts  18.2 us
    pallas_call x2, Pallas kernels, cross_products(): pl.pallas_call(functools.partial(cross_kernel, side, orders), grid=(size...  12.9 us
    dot_general x7, matrix products, dot(): lax.dot_general(x, y, (contract, ((), ())), preferred_element_type=jnp.fl...  11.4 us
    all_to_all x2, starting transfers between devices, exchange(): lax.all_to_all(x, 'dp', split_axis=0, concat_axis=0, axis_index_groups=gr...  9.74 us
  transfers between devices with their start and end apart: 63, of which 27 were waited for; matrix products, arithmetic and copies ran while one was open for 7% of the time, Pallas kernels for 8%

commit v1 on v0

--- a/solution.py
+++ b/solution.py
@@ -358,7 +358,7 @@
 
     own_b = exchange(eighths)
     far_1 = [turn(x[:, half:], s + 1) for s, x in enumerate(parts_a[1:])]
-    for mask in [1] + h_masks:
+    for mask in h_masks + [1]:
         sums = sums + swap(sums, mask)
     rest, arrived, sums, pieces_b, near, parts_a, far_1 = together(
         (rest, arrived, sums, pieces_b, near, parts_a, far_1)
@@ -537,6 +537,8 @@
     for step in (1, 2):
         sibling.append([swap(x, 1) for x in turned[step]])
     loss = jnp.broadcast_to(stats_a[2:3, :128], (8, 128))
+    for mask in h_masks:
+        stats_b = stats_b + swap(stats_b, mask)
     first_a = stats_a[0:1] / count
     second_a = line_a[0] * stats_a[1:2] + line_a[1] * first_a
     all_a = jnp.concatenate([parts_a[0][:, :half]] + far_0 + [other_a], 0)
@@ -544,8 +546,8 @@
         1, norm_b, arrived, orders, k, cross, all_a, mean_ah, inv_ah, first_a, second_a
     )
     out_a, stats_b, sibling, rest, loss = together((out_a, stats_b, sibling, rest, loss))
-    for mask in h_masks:
-        stats_b = stats_b + swap(stats_b, mask)
+    stats_b = stats_b + swap(stats_b, 1)
+    loss = loss + swap(loss, 1)
 
     for s in range(1, cubes):
         for side, blocks in enumerate((turned, sibling)):
@@ -556,8 +558,6 @@
     mine = cubes * rows
     both = jnp.concatenate([out_a[:mine], swap(out_a[mine:], 1)], 1)
     both, grad_nb, loss, stats_b = together((both, grad_nb, loss, stats_b))
-    stats_b = stats_b + swap(stats_b, 1)
-    loss = loss + swap(loss, 1)
     first_b = stats_b[0:1] / count
     second_b = line_b[0] * stats_b[1:2] + line_b[1] * first_b
     for mask in h_masks:

time: 313 us -> 310 us (level)
  waiting for transfers between devices: 156 us -> 152 us
    ppermute x49, waiting for transfers between devices: 98.1 us -> 93.6 us  [swap(): return lax.ppermute(x, 'dp', [(i, i ^ mask) for i in range(devices)])]
  transfers between devices with their start and end apart: 63 -> 63, of which waited for: 27 -> 25; matrix products, arithmetic and copies ran while one was open for 7% -> 7% of each run, Pallas kernels for 8% -> 8%
where the time goes in v1:
time: 310 us; the launch traced here: 308 us
  waiting for transfers between devices  152 us (49%)
  starting transfers between devices  77.6 us (25%)
  Pallas kernels  31.7 us (10%)
  local copies, waits for them, and re-layouts  20.5 us (7%)
  other arithmetic  12.5 us (4%)
  matrix products  11.4 us (4%)
    ppermute x49, waiting for transfers between devices, swap(): return lax.ppermute(x, 'dp', [(i, i ^ mask) for i in range(devices)])  93.6 us
    ppermute x12, waiting for transfers between devices, turn(): lax.ppermute(x, 'dp', [(i, (i + 2 * cube * step) % devices) for i in rang...  58.6 us
    ppermute x49, starting transfers between devices, swap(): return lax.ppermute(x, 'dp', [(i, i ^ mask) for i in range(devices)])  48 us
    ppermute x12, starting transfers between devices, turn(): lax.ppermute(x, 'dp', [(i, (i + 2 * cube * step) % devices) for i in rang...  19.8 us
    unnamed x95, local copies, waits for them, and re-layouts  17.8 us
    pallas_call x2, Pallas kernels, cross_products(): pl.pallas_call(functools.partial(cross_kernel, side, orders), grid=(size...  12.9 us
    dot_general x7, matrix products, dot(): lax.dot_general(x, y, (contract, ((), ())), preferred_element_type=jnp.fl...  11.4 us
    all_to_all x2, starting transfers between devices, exchange(): lax.all_to_all(x, 'dp', split_axis=0, concat_axis=0, axis_index_groups=gr...  9.74 us
  transfers between devices with their start and end apart: 63, of which 25 were waited for; matrix products, arithmetic and copies ran while one was open for 7% of the time, Pallas kernels for 8%

profile of v1, /device:TPU:0, one launch (start us, length us, event | category | flops | bytes accessed | tf_op | source)
XLA Modules:
  0.0 307.5 jit_solution(3543871258649020319)
XLA Ops:
  3.2 2.1 shard_map.49
  8.6 6.2 %all-to-all-start = ((bf16[8,128,512]{2,1,0:T(8,128)(2,1)}), bf16[8,128,512]{2,1,0:T(8,128)(2,1)S(1)}, u32[]{:S(2)}, u32[]{:S(2)}) async-start(bf16[8,128,512]{2,1,0:T(8,128)(2,1)} %get-tuple-element.210), calls=%async_computation | async-start | bytes 2097152 | tf_op jit(solution)/shard_map/all_to_all | solution.py:334
  14.8 2.7 collective-permute-start.3
  17.5 2.0 collective-permute-start.2
  22.8 6.1 %collective-permute-done.3 = f32[4,4096]{1,0:T(4,128)S(1)} collective-permute-done((f32[4,4096]{1,0:T(4,128)}, f32[4,4096]{1,0:T(4,128)S(1)}, u32[]{:S(2)}, u32[]{:S(2)}) %collective-permute-start.3) | collective-permute-done | bytes 65568 | tf_op jit(solution)/shard_map/ppermute | solution.py:320
  31.1 8.6 %collective-permute-done.refs_3_ = bf16[128,768]{1,0:T(8,128)(2,1)S(1)} collective-permute-done((bf16[128,768]{1,0:T(8,128)(2,1)S(1)}, bf16[128,768]{1,0:T(8,128)(2,1)S(1)}, u32[]{:S(2)}, u32[]{:S(2)}) %collective-permute-start) | collective-permute-done | bytes 196640 | tf_op jit(solution)/shard_map/ppermute | solution.py:320
  42.8 1.8 collective-permute-start.6
  44.6 1.8 collective-permute-start.7
  49.1 4.7 %collective-permute-done.10 = f32[4,4096]{1,0:T(4,128)S(1)} collective-permute-done((f32[4,4096]{1,0:T(4,128)S(1)}, f32[4,4096]{1,0:T(4,128)S(1)}, u32[]{:S(2)}, u32[]{:S(2)}) %collective-permute-start.10) | collective-permute-done | bytes 65568 | tf_op jit(solution)/shard_map/ppermute | solution.py:320
  54.5 3.7 %collective-permute-done.11 = f32[4,4096]{1,0:T(4,128)S(1)} collective-permute-done((f32[4,4096]{1,0:T(4,128)S(1)}, f32[4,4096]{1,0:T(4,128)S(1)}, u32[]{:S(2)}, u32[]{:S(2)}) %collective-permute-start.11) | collective-permute-done | bytes 65568 | tf_op jit(solution)/shard_map/ppermute | solution.py:320
  61.0 3.8 %collective-permute-done.9 = bf16[64,4096]{1,0:T(8,128)(2,1)} collective-permute-done((bf16[64,4096]{1,0:T(8,128)(2,1)S(1)}, bf16[64,4096]{1,0:T(8,128)(2,1)}, u32[]{:S(2)}, u32[]{:S(2)}) %collective-permute-start.9) | collective-permute-done | bytes 524320 | tf_op jit(solution)/shard_map/ppermute | solution.py:326
  69.9 2.1 collective-permute-start.14
  72.0 3.7 %collective-permute-start.15 = (bf16[64,4096]{1,0:T(8,128)(2,1)S(1)}, bf16[64,4096]{1,0:T(8,128)(2,1)S(1)}, u32[]{:S(2)}, u32[]{:S(2)}) collective-permute-start(bf16[64,4096]{1,0:T(8,128)(2,1)S(1)} %copy-done.31), channel_id=1, source_target_pairs={{0,16},{1,17},{2,18},{3,19},{4,20},{5,21},{6,22},{7,23},{8,24},{9,... | collective-permute-start | bytes 1572872 | tf_op jit(solution)/shard_map/ppermute | solution.py:326
  79.3 14.5 %collective-permute-done.14.refs_5_ = bf16[512,512]{1,0:T(8,128)(2,1)S(1)} collective-permute-done((bf16[512,512]{1,0:T(8,128)(2,1)S(1)}, bf16[512,512]{1,0:T(8,128)(2,1)S(1)}, u32[]{:S(2)}, u32[]{:S(2)}) %collective-permute-start.14) | collective-permute-done | bytes 524320 | tf_op jit(solution)/shard_map/ppermute | solution.py:320
  93.9 1.5 shard_map.53
  98.4 3.5 %collective-permute-start.18 = (bf16[128,768]{1,0:T(8,128)(2,1)S(1)}, bf16[128,768]{1,0:T(8,128)(2,1)S(1)}, u32[]{:S(2)}, u32[]{:S(2)}) collective-permute-start(bf16[128,768]{1,0:T(8,128)(2,1)S(1)} %copy-done.14), channel_id=1, source_target_pairs={{0,8},{1,9},{2,10},{3,11},{4,12},{5,13},{6,14},{7,15},{8,0},{9,1},... | collective-permute-start | bytes 589832 | tf_op jit(solution)/shard_map/ppermute | solution.py:320
  105.3 1.8 collective-permute-done.18.refs_3_
  108.6 2.8 collective-permute-start.24
  115.6 4.0 %shard_map.55 = f32[4,2048]{1,0:T(4,128)S(1)} custom-call(f32[1,2048]{1,0:T(1,128)S(1)} %get-tuple-element.410.mean_ref, f32[1,2048]{1,0:T(1,128)S(1)} %get-tuple-element.408.inv_ref, bf16[512,768]{1,0:T(8,128)(2,1)S(1)} %get-tuple-element.262.refs_0_, bf16[512,768]{1,0:T(8,128)(2,1)S(1)} %collective-permute-done.12.refs_1_, ...), custom_call_target="tpu_custom_call" | custom-call | tf_op jit(solution)/shard_map/pallas_call | solution.py:169
  119.7 2.9 collective-permute-done.23.refs_5_
  122.6 5.7 %collective-permute-done.24 = bf16[192,1024]{1,0:T(8,128)(2,1)S(1)} collective-permute-done((bf16[192,1024]{1,0:T(8,128)(2,1)S(1)}, bf16[192,1024]{1,0:T(8,128)(2,1)S(1)}, u32[]{:S(2)}, u32[]{:S(2)}) %collective-permute-start.24) | collective-permute-done | bytes 393248 | tf_op jit(solution)/shard_map/ppermute | solution.py:326
  128.2 1.6 collective-permute-done.22.refs_4_
  130.0 3.0 collective-permute-start.30
  136.2 1.6 multiply_convert_fusion
  137.8 7.7 %collective-permute-done.31 = f32[4,2560]{1,0:T(4,128)S(1)} collective-permute-done((f32[4,2560]{1,0:T(4,128)S(1)}, f32[4,2560]{1,0:T(4,128)S(1)}, u32[]{:S(2)}, u32[]{:S(2)}) %collective-permute-start.31) | collective-permute-done | bytes 40992 | tf_op jit(solution)/shard_map/ppermute | solution.py:326
  145.5 10.0 %collective-permute-done.30 = bf16[256,1024]{1,0:T(8,128)(2,1)S(1)} collective-permute-done((bf16[256,1024]{1,0:T(8,128)(2,1)S(1)}, bf16[256,1024]{1,0:T(8,128)(2,1)S(1)}, u32[]{:S(2)}, u32[]{:S(2)}) %collective-permute-start.30) | collective-permute-done | bytes 524320 | tf_op jit(solution)/shard_map/ppermute | solution.py:326
  155.6 1.5 shard_map.57
  160.4 1.6 collective-permute-start.33
  163.2 2.3 pad_maximum_fusion.rows_ref
  166.0 3.4 %collective-permute-done.33 = bf16[64,1024]{1,0:T(8,128)(2,1)S(1)} collective-permute-done((bf16[64,1024]{1,0:T(8,128)(2,1)S(1)}, bf16[64,1024]{1,0:T(8,128)(2,1)S(1)}, u32[]{:S(2)}, u32[]{:S(2)}) %collective-permute-start.33) | collective-permute-done | bytes 131104 | tf_op jit(solution)/shard_map/ppermute | solution.py:326
  169.8 2.6 fusion.6
  176.1 2.4 collective-permute-start.36
  178.5 4.0 %shard_map.58 = f32[4,2048]{1,0:T(4,128)S(1)} custom-call(f32[1,2048]{1,0:T(1,128)S(1)} %get-tuple-element.411.mean_ref, f32[1,2048]{1,0:T(1,128)S(1)} %get-tuple-element.409.inv_ref, bf16[512,768]{1,0:T(8,128)(2,1)S(1)} %get-tuple-element.304.refs_0_, bf16[512,768]{1,0:T(8,128)(2,1)S(1)} %collective-permute-done.27.refs_1_, ...), custom_call_target="tpu_custom_call" | custom-call | tf_op jit(solution)/shard_map/pallas_call | solution.py:169
  184.1 2.3 collective-permute-done.41
  186.5 7.8 %collective-permute-done.39 = bf16[192,1024]{1,0:T(8,128)(2,1)S(1)} collective-permute-done((bf16[192,1024]{1,0:T(8,128)(2,1)S(1)}, bf16[192,1024]{1,0:T(8,128)(2,1)S(1)}, u32[]{:S(2)}, u32[]{:S(2)}) %collective-permute-start.39) | collective-permute-done | bytes 393248 | tf_op jit(solution)/shard_map/ppermute | solution.py:326
  198.8 2.4 collective-permute-start.45
  202.4 20.4 %collective-permute-done.45 = bf16[192,1024]{1,0:T(8,128)(2,1)S(1)} collective-permute-done((bf16[192,1024]{1,0:T(8,128)(2,1)S(1)}, bf16[192,1024]{1,0:T(8,128)(2,1)S(1)}, u32[]{:S(2)}, u32[]{:S(2)}) %collective-permute-start.45) | collective-permute-done | bytes 393248 | tf_op jit(solution)/shard_map/ppermute | solution.py:326
  222.7 2.2 collective-permute-done.43.refs_4_
  228.6 3.7 %fusion.62 = f32[1024,512]{1,0:T(8,128)} fusion(bf16[1024,2048]{1,0:T(8,128)(2,1)S(1)} %shard_map.57, bf16[512,2048]{1,0:T(8,128)(2,1)S(1)} %pad_maximum_fusion.1), kind=kOutput, calls=%fused_computation.125 | convolution fusion | flops 2147483648 | bytes 8388608 | tf_op jit(solution)/shard_map/dot_general | solution.py:250
  232.3 1.8 collective-permute-start.51
  235.2 6.6 %shard_map.61.refs_0_ = f32[512,1024]{1,0:T(8,128)} custom-call(s32[1]{0:T(128)} %bitcast.k_ref, bf16[512,4096]{1,0:T(8,128)(2,1)} %pad_maximum_fusion.rows_ref, bf16[2048,384]{1,0:T(8,128)(2,1)S(1)} %get-tuple-element.332.refs_0_, bf16[2048,384]{1,0:T(8,128)(2,1)S(1)} %get-tuple-element.333.refs_1_, bf16[2048,256]{1,0:T(8,128)(2,1)S(1)} %get-tuple-element.334.refs_2_), custom_call_target="tpu_custom_call" | custom-call | flops 2147483648 | bytes 8388608 | tf_op jit(solution)/shard_map/pallas_call | solution.py:293
  241.8 20.1 %collective-permute-done.52 = f32[3,1024]{1,0:T(4,128)S(1)} collective-permute-done((f32[3,1024]{1,0:T(4,128)S(1)}, f32[3,1024]{1,0:T(4,128)S(1)}, u32[]{:S(2)}, u32[]{:S(2)}) %collective-permute-start.52) | collective-permute-done | bytes 12320 | tf_op jit(solution)/shard_map/ppermute | solution.py:320
  265.4 6.3 %shard_map.62 = bf16[512,1024]{1,0:T(8,128)(2,1)S(1)} custom-call(s32[1]{0:T(128)} %bitcast.k_ref, bf16[512,4096]{1,0:T(8,128)(2,1)} %pad_maximum_fusion.rows_ref, f32[512,1024]{1,0:T(8,128)} %shard_map.61.refs_0_, bf16[512,1024]{1,0:T(8,128)(2,1)S(1)} %pad_maximum_fusion.3.refs_1_, f32[1,1024]{1,0:T(1,128)S(1)} %slice.246.refs_2_, ...), custom_call_target="tpu_custom_call" | custom-call | flops 2147483648 | bytes 8388608 | tf_op jit(solution)/shard_map/pallas_call | solution.py:293
  275.7 1.7 shard_map.64
  277.4 3.6 %all-to-all-start.1 = ((bf16[8,128,512]{2,1,0:T(8,128)(2,1)}), bf16[8,128,512]{2,1,0:T(8,128)(2,1)S(1)}, u32[]{:S(2)}, u32[]{:S(2)}) async-start(bf16[8,128,512]{2,1,0:T(8,128)(2,1)} %shard_map.64), calls=%async_computation.1 | async-start | bytes 2097152 | tf_op jit(solution)/shard_map/all_to_all | solution.py:334
  281.1 1.6 collective-permute-start.60
  284.1 20.2 %collective-permute-done.59 = f32[8,128]{1,0:T(8,128)S(1)} collective-permute-done((f32[8,128]{1,0:T(8,128)S(1)}, f32[8,128]{1,0:T(8,128)S(1)}, u32[]{:S(2)}, u32[]{:S(2)}) %collective-permute-start.59) | collective-permute-done | bytes 4128 | tf_op jit(solution)/shard_map/ppermute | solution.py:320
  304.8 1.6 shard_map.63
  (273 shorter events, 76.4 us)
Async XLA Ops:
  8.6 56.2 %all-to-all-start = ((bf16[8,128,512]{2,1,0:T(8,128)(2,1)}), bf16[8,128,512]{2,1,0:T(8,128)(2,1)S(1)}, u32[]{:S(2)}, u32[]{:S(2)}) async-start(bf16[8,128,512]{2,1,0:T(8,128)(2,1)} %get-tuple-element.210), calls=%async_computation | async-start | bytes 2097152 | tf_op jit(solution)/shard_map/all_to_all | solution.py:334
  14.8 14.0 %collective-permute-start.3 = (f32[4,4096]{1,0:T(4,128)}, f32[4,4096]{1,0:T(4,128)S(1)}, u32[]{:S(2)}, u32[]{:S(2)}) collective-permute-start(f32[4,4096]{1,0:T(4,128)} %copy-done.25), channel_id=1, source_target_pairs={{0,16},{1,17},{2,18},{3,19},{4,20},{5,21},{6,22},{7,23},{8,24},{9,... | collective-permute-start | bytes 196616 | tf_op jit(solution)/shard_map/ppermute | solution.py:320
  17.5 13.6 %collective-permute-start.2 = (bf16[128,512]{1,0:T(8,128)(2,1)}, bf16[128,512]{1,0:T(8,128)(2,1)S(1)}, u32[]{:S(2)}, u32[]{:S(2)}) collective-permute-start(bf16[128,512]{1,0:T(8,128)(2,1)} %copy-done.23), channel_id=1, source_target_pairs={{0,4},{1,5},{2,6},{3,7},{4,0},{5,1},{6,2},{7,3},{8,12},{9,13},{10,... | collective-permute-start | bytes 393224 | tf_op jit(solution)/shard_map/ppermute | solution.py:320
  19.4 20.2 %collective-permute-start = (bf16[128,768]{1,0:T(8,128)(2,1)S(1)}, bf16[128,768]{1,0:T(8,128)(2,1)S(1)}, u32[]{:S(2)}, u32[]{:S(2)}) collective-permute-start(bf16[128,768]{1,0:T(8,128)(2,1)S(1)} %get-tuple-element.198.refs_0_), channel_id=1, source_target_pairs={{0,8},{1,9},{2,10},{3,11},{4,12},{5,13},{6,14},{7,15},{8,0},{9,1},... | collective-permute-start | bytes 589832 | tf_op jit(solution)/shard_map/ppermute | solution.py:320
  20.9 18.8 %collective-permute-start.1 = (bf16[128,768]{1,0:T(8,128)(2,1)S(1)}, bf16[128,768]{1,0:T(8,128)(2,1)S(1)}, u32[]{:S(2)}, u32[]{:S(2)}) collective-permute-start(bf16[128,768]{1,0:T(8,128)(2,1)S(1)} %get-tuple-element.199.refs_1_), channel_id=1, source_target_pairs={{0,2},{1,3},{2,0},{3,1},{4,6},{5,7},{6,4},{7,5},{8,10},{9,11},{10,... | collective-permute-start | bytes 589832 | tf_op jit(solution)/shard_map/ppermute | solution.py:320
  22.4 17.3 %collective-permute-start.5 = (bf16[128,1024]{1,0:T(8,128)(2,1)S(1)}, bf16[128,1024]{1,0:T(8,128)(2,1)S(1)}, u32[]{:S(2)}, u32[]{:S(2)}) collective-permute-start(bf16[128,1024]{1,0:T(8,128)(2,1)S(1)} %slice.213), channel_id=1, source_target_pairs={{0,16},{1,17},{2,18},{3,19},{4,20},{5,21},{6,22},{7,23},{8,24},{9,... | collective-permute-start | bytes 786440 | tf_op jit(solution)/shard_map/ppermute | solution.py:326
  39.6 25.1 %collective-permute-start.9 = (bf16[64,4096]{1,0:T(8,128)(2,1)S(1)}, bf16[64,4096]{1,0:T(8,128)(2,1)}, u32[]{:S(2)}, u32[]{:S(2)}) collective-permute-start(bf16[64,4096]{1,0:T(8,128)(2,1)S(1)} %get-tuple-element.207), channel_id=1, source_target_pairs={{0,16},{1,17},{2,18},{3,19},{4,20},{5,21},{6,22},{7,23},{8,24},{9,... | collective-permute-start | bytes 1572872 | tf_op jit(solution)/shard_map/ppermute | solution.py:326
  42.8 16.7 %collective-permute-start.6 = (bf16[256,768]{1,0:T(8,128)(2,1)S(1)}, bf16[256,768]{1,0:T(8,128)(2,1)S(1)}, u32[]{:S(2)}, u32[]{:S(2)}) collective-permute-start(bf16[256,768]{1,0:T(8,128)(2,1)S(1)} %get-tuple-element.214.refs_0_), channel_id=1, source_target_pairs={{0,4},{1,5},{2,6},{3,7},{4,0},{5,1},{6,2},{7,3},{8,12},{9,13},{10,... | collective-permute-start | bytes 1179656 | tf_op jit(solution)/shard_map/ppermute | solution.py:320
  44.6 15.7 %collective-permute-start.7 = (bf16[256,768]{1,0:T(8,128)(2,1)S(1)}, bf16[256,768]{1,0:T(8,128)(2,1)S(1)}, u32[]{:S(2)}, u32[]{:S(2)}) collective-permute-start(bf16[256,768]{1,0:T(8,128)(2,1)S(1)} %get-tuple-element.215.refs_1_), channel_id=1, source_target_pairs={{0,8},{1,9},{2,10},{3,11},{4,12},{5,13},{6,14},{7,15},{8,0},{9,1},... | collective-permute-start | bytes 1179656 | tf_op jit(solution)/shard_map/ppermute | solution.py:320
  46.4 12.4 %collective-permute-start.8 = (bf16[256,512]{1,0:T(8,128)(2,1)S(1)}, bf16[256,512]{1,0:T(8,128)(2,1)S(1)}, u32[]{:S(2)}, u32[]{:S(2)}) collective-permute-start(bf16[256,512]{1,0:T(8,128)(2,1)S(1)} %get-tuple-element.216.refs_2_), channel_id=1, source_target_pairs={{0,2},{1,3},{2,0},{3,1},{4,6},{5,7},{6,4},{7,5},{8,10},{9,11},{10,... | collective-permute-start | bytes 786440 | tf_op jit(solution)/shard_map/ppermute | solution.py:320
  64.8 12.9 %collective-permute-start.16 = (f32[4,4096]{1,0:T(4,128)}, f32[4,4096]{1,0:T(4,128)}, u32[]{:S(2)}, u32[]{:S(2)}) collective-permute-start(f32[4,4096]{1,0:T(4,128)} %add.164), channel_id=1, source_target_pairs={{0,8},{1,9},{2,10},{3,11},{4,12},{5,13},{6,14},{7,15},{8,0},{9,1},... | collective-permute-start | bytes 196616 | tf_op jit(solution)/shard_map/ppermute | solution.py:320
  69.9 23.9 %collective-permute-start.14 = (bf16[512,512]{1,0:T(8,128)(2,1)S(1)}, bf16[512,512]{1,0:T(8,128)(2,1)S(1)}, u32[]{:S(2)}, u32[]{:S(2)}) collective-permute-start(bf16[512,512]{1,0:T(8,128)(2,1)S(1)} %get-tuple-element.266.refs_4_), channel_id=1, source_target_pairs={{0,8},{1,9},{2,10},{3,11},{4,12},{5,13},{6,14},{7,15},{8,0},{9,1},... | collective-permute-start | bytes 1572872 | tf_op jit(solution)/shard_map/ppermute | solution.py:320
  72.0 21.9 %collective-permute-start.15 = (bf16[64,4096]{1,0:T(8,128)(2,1)S(1)}, bf16[64,4096]{1,0:T(8,128)(2,1)S(1)}, u32[]{:S(2)}, u32[]{:S(2)}) collective-permute-start(bf16[64,4096]{1,0:T(8,128)(2,1)S(1)} %copy-done.31), channel_id=1, source_target_pairs={{0,16},{1,17},{2,18},{3,19},{4,20},{5,21},{6,22},{7,23},{8,24},{9,... | collective-permute-start | bytes 1572872 | tf_op jit(solution)/shard_map/ppermute | solution.py:326
  75.7 18.2 %collective-permute-start.12 = (bf16[512,768]{1,0:T(8,128)(2,1)S(1)}, bf16[512,768]{1,0:T(8,128)(2,1)S(1)}, u32[]{:S(2)}, u32[]{:S(2)}) collective-permute-start(bf16[512,768]{1,0:T(8,128)(2,1)S(1)} %get-tuple-element.262.refs_0_), channel_id=1, source_target_pairs={{0,2},{1,3},{2,0},{3,1},{4,6},{5,7},{6,4},{7,5},{8,10},{9,11},{10,... | collective-permute-start | bytes 2359304 | tf_op jit(solution)/shard_map/ppermute | solution.py:320
  77.1 16.7 %collective-permute-start.13 = (bf16[512,768]{1,0:T(8,128)(2,1)S(1)}, bf16[512,768]{1,0:T(8,128)(2,1)S(1)}, u32[]{:S(2)}, u32[]{:S(2)}) collective-permute-start(bf16[512,768]{1,0:T(8,128)(2,1)S(1)} %get-tuple-element.264.refs_2_), channel_id=1, source_target_pairs={{0,4},{1,5},{2,6},{3,7},{4,0},{5,1},{6,2},{7,3},{8,12},{9,13},{10,... | collective-permute-start | bytes 2359304 | tf_op jit(solution)/shard_map/ppermute | solution.py:320
  96.8 8.0 %collective-permute-start.17 = (f32[512,1024]{1,0:T(8,128)S(1)}, f32[512,1024]{1,0:T(8,128)S(1)}, u32[]{:S(2)}, u32[]{:S(2)}) collective-permute-start(f32[512,1024]{1,0:T(8,128)S(1)} %fusion.13), channel_id=1, source_target_pairs={{0,1},{1,0},{2,3},{3,2},{4,5},{5,4},{6,7},{7,6},{8,9},{9,8},{10,11... | collective-permute-start | bytes 6291464 | tf_op jit(solution)/shard_map/ppermute | solution.py:320
  96.9 8.4 %collective-permute-start.20 = (bf16[128,512]{1,0:T(8,128)(2,1)S(1)}, bf16[128,512]{1,0:T(8,128)(2,1)S(1)}, u32[]{:S(2)}, u32[]{:S(2)}) collective-permute-start(bf16[128,512]{1,0:T(8,128)(2,1)S(1)} %copy-done.22), channel_id=1, source_target_pairs={{0,4},{1,5},{2,6},{3,7},{4,0},{5,1},{6,2},{7,3},{8,12},{9,13},{10,... | collective-permute-start | bytes 393224 | tf_op jit(solution)/shard_map/ppermute | solution.py:320
  98.4 8.7 %collective-permute-start.18 = (bf16[128,768]{1,0:T(8,128)(2,1)S(1)}, bf16[128,768]{1,0:T(8,128)(2,1)S(1)}, u32[]{:S(2)}, u32[]{:S(2)}) collective-permute-start(bf16[128,768]{1,0:T(8,128)(2,1)S(1)} %copy-done.14), channel_id=1, source_target_pairs={{0,8},{1,9},{2,10},{3,11},{4,12},{5,13},{6,14},{7,15},{8,0},{9,1},... | collective-permute-start | bytes 589832 | tf_op jit(solution)/shard_map/ppermute | solution.py:320
  103.4 16.3 %collective-permute-start.25 = (bf16[256,1024]{1,0:T(8,128)(2,1)S(1)}, bf16[256,1024]{1,0:T(8,128)(2,1)S(1)}, u32[]{:S(2)}, u32[]{:S(2)}) collective-permute-start(bf16[256,1024]{1,0:T(8,128)(2,1)S(1)} %pad_maximum_fusion.5), channel_id=1, source_target_pairs={{0,1},{1,0},{2,3},{3,2},{4,5},{5,4},{6,7},{7,6},{8,9},{9,8},{10,11... | collective-permute-start | bytes 1572872 | tf_op jit(solution)/shard_map/ppermute | solution.py:320
  108.6 19.6 %collective-permute-start.24 = (bf16[192,1024]{1,0:T(8,128)(2,1)S(1)}, bf16[192,1024]{1,0:T(8,128)(2,1)S(1)}, u32[]{:S(2)}, u32[]{:S(2)}) collective-permute-start(bf16[192,1024]{1,0:T(8,128)(2,1)S(1)} %slice.224), channel_id=1, source_target_pairs={{0,16},{1,17},{2,18},{3,19},{4,20},{5,21},{6,22},{7,23},{8,24},{9,... | collective-permute-start | bytes 1179656 | tf_op jit(solution)/shard_map/ppermute | solution.py:326
  111.5 16.8 %collective-permute-start.21 = (bf16[256,768]{1,0:T(8,128)(2,1)S(1)}, bf16[256,768]{1,0:T(8,128)(2,1)S(1)}, u32[]{:S(2)}, u32[]{:S(2)}) collective-permute-start(bf16[256,768]{1,0:T(8,128)(2,1)S(1)} %get-tuple-element.269.refs_0_), channel_id=1, source_target_pairs={{0,4},{1,5},{2,6},{3,7},{4,0},{5,1},{6,2},{7,3},{8,12},{9,13},{10,... | collective-permute-start | bytes 1179656 | tf_op jit(solution)/shard_map/ppermute | solution.py:320
  112.1 17.7 %collective-permute-start.22 = (bf16[256,768]{1,0:T(8,128)(2,1)S(1)}, bf16[256,768]{1,0:T(8,128)(2,1)S(1)}, u32[]{:S(2)}, u32[]{:S(2)}) collective-permute-start(bf16[256,768]{1,0:T(8,128)(2,1)S(1)} %get-tuple-element.270.refs_1_), channel_id=1, source_target_pairs={{0,8},{1,9},{2,10},{3,11},{4,12},{5,13},{6,14},{7,15},{8,0},{9,1},... | collective-permute-start | bytes 1179656 | tf_op jit(solution)/shard_map/ppermute | solution.py:320
  114.2 8.4 %collective-permute-start.23 = (bf16[256,512]{1,0:T(8,128)(2,1)S(1)}, bf16[256,512]{1,0:T(8,128)(2,1)S(1)}, u32[]{:S(2)}, u32[]{:S(2)}) collective-permute-start(bf16[256,512]{1,0:T(8,128)(2,1)S(1)} %get-tuple-element.271.refs_2_), channel_id=1, source_target_pairs={{0,2},{1,3},{2,0},{3,1},{4,6},{5,7},{6,4},{7,5},{8,10},{9,11},{10,... | collective-permute-start | bytes 786440 | tf_op jit(solution)/shard_map/ppermute | solution.py:320
  129.9 15.6 %collective-permute-start.31 = (f32[4,2560]{1,0:T(4,128)S(1)}, f32[4,2560]{1,0:T(4,128)S(1)}, u32[]{:S(2)}, u32[]{:S(2)}) collective-permute-start(f32[4,2560]{1,0:T(4,128)S(1)} %pad_maximum_fusion.7), channel_id=1, source_target_pairs={{0,16},{1,17},{2,18},{3,19},{4,20},{5,21},{6,22},{7,23},{8,24},{9,... | collective-permute-start | bytes 122888 | tf_op jit(solution)/shard_map/ppermute | solution.py:326
  130.0 25.4 %collective-permute-start.30 = (bf16[256,1024]{1,0:T(8,128)(2,1)S(1)}, bf16[256,1024]{1,0:T(8,128)(2,1)S(1)}, u32[]{:S(2)}, u32[]{:S(2)}) collective-permute-start(bf16[256,1024]{1,0:T(8,128)(2,1)S(1)} %slice.226), channel_id=1, source_target_pairs={{0,16},{1,17},{2,18},{3,19},{4,20},{5,21},{6,22},{7,23},{8,24},{9,... | collective-permute-start | bytes 1572872 | tf_op jit(solution)/shard_map/ppermute | solution.py:326
  133.2 22.3 %collective-permute-start.29 = (bf16[512,512]{1,0:T(8,128)(2,1)S(1)}, bf16[512,512]{1,0:T(8,128)(2,1)S(1)}, u32[]{:S(2)}, u32[]{:S(2)}) collective-permute-start(bf16[512,512]{1,0:T(8,128)(2,1)S(1)} %get-tuple-element.308.refs_4_), channel_id=1, source_target_pairs={{0,8},{1,9},{2,10},{3,11},{4,12},{5,13},{6,14},{7,15},{8,0},{9,1},... | collective-permute-start | bytes 1572872 | tf_op jit(solution)/shard_map/ppermute | solution.py:320
  133.3 22.2 %collective-permute-start.27 = (bf16[512,768]{1,0:T(8,128)(2,1)S(1)}, bf16[512,768]{1,0:T(8,128)(2,1)S(1)}, u32[]{:S(2)}, u32[]{:S(2)}) collective-permute-start(bf16[512,768]{1,0:T(8,128)(2,1)S(1)} %get-tuple-element.304.refs_0_), channel_id=1, source_target_pairs={{0,2},{1,3},{2,0},{3,1},{4,6},{5,7},{6,4},{7,5},{8,10},{9,11},{10,... | collective-permute-start | bytes 2359304 | tf_op jit(solution)/shard_map/ppermute | solution.py:320
  134.8 20.7 %collective-permute-start.28 = (bf16[512,768]{1,0:T(8,128)(2,1)S(1)}, bf16[512,768]{1,0:T(8,128)(2,1)S(1)}, u32[]{:S(2)}, u32[]{:S(2)}) collective-permute-start(bf16[512,768]{1,0:T(8,128)(2,1)S(1)} %get-tuple-element.306.refs_2_), channel_id=1, source_target_pairs={{0,4},{1,5},{2,6},{3,7},{4,0},{5,1},{6,2},{7,3},{8,12},{9,13},{10,... | collective-permute-start | bytes 2359304 | tf_op jit(solution)/shard_map/ppermute | solution.py:320
  155.5 7.8 %collective-permute-start.35 = (bf16[256,4096]{1,0:T(8,128)(2,1)S(1)}, bf16[256,4096]{1,0:T(8,128)(2,1)S(1)}, u32[]{:S(2)}, u32[]{:S(2)}) collective-permute-start(bf16[256,4096]{1,0:T(8,128)(2,1)S(1)} %multiply_convert_fusion), channel_id=1, source_target_pairs={{0,1},{1,0},{2,3},{3,2},{4,5},{5,4},{6,7},{7,6},{8,9},{9,8},{10,11... | collective-permute-start | bytes 6291464 | tf_op jit(solution)/shard_map/ppermute | solution.py:320
  160.4 9.0 %collective-permute-start.33 = (bf16[64,1024]{1,0:T(8,128)(2,1)S(1)}, bf16[64,1024]{1,0:T(8,128)(2,1)S(1)}, u32[]{:S(2)}, u32[]{:S(2)}) collective-permute-start(bf16[64,1024]{1,0:T(8,128)(2,1)S(1)} %slice.229), channel_id=1, source_target_pairs={{0,16},{1,17},{2,18},{3,19},{4,20},{5,21},{6,22},{7,23},{8,24},{9,... | collective-permute-start | bytes 393224 | tf_op jit(solution)/shard_map/ppermute | solution.py:326
  173.2 9.3 %collective-permute-start.40 = (f32[3,1024]{1,0:T(4,128)S(1)}, f32[3,1024]{1,0:T(4,128)S(1)}, u32[]{:S(2)}, u32[]{:S(2)}) collective-permute-start(f32[3,1024]{1,0:T(4,128)S(1)} %maximum_maximum_fusion), channel_id=1, source_target_pairs={{0,2},{1,3},{2,0},{3,1},{4,6},{5,7},{6,4},{7,5},{8,10},{9,11},{10,... | collective-permute-start | bytes 36872 | tf_op jit(solution)/shard_map/ppermute | solution.py:320
  174.9 11.6 %collective-permute-start.38 = (bf16[512,256]{1,0:T(8,128)(2,1)S(1)}, bf16[512,256]{1,0:T(8,128)(2,1)S(1)}, u32[]{:S(2)}, u32[]{:S(2)}) collective-permute-start(bf16[512,256]{1,0:T(8,128)(2,1)S(1)} %slice.286.refs_2_), channel_id=1, source_target_pairs={{0,4},{1,5},{2,6},{3,7},{4,0},{5,1},{6,2},{7,3},{8,12},{9,13},{10,... | collective-permute-start | bytes 786440 | tf_op jit(solution)/shard_map/ppermute | solution.py:320
  175.5 18.7 %collective-permute-start.39 = (bf16[192,1024]{1,0:T(8,128)(2,1)S(1)}, bf16[192,1024]{1,0:T(8,128)(2,1)S(1)}, u32[]{:S(2)}, u32[]{:S(2)}) collective-permute-start(bf16[192,1024]{1,0:T(8,128)(2,1)S(1)} %slice.287), channel_id=1, source_target_pairs={{0,16},{1,17},{2,18},{3,19},{4,20},{5,21},{6,22},{7,23},{8,24},{9,... | collective-permute-start | bytes 1179656 | tf_op jit(solution)/shard_map/ppermute | solution.py:326
  175.5 18.7 %collective-permute-start.37 = (bf16[512,384]{1,0:T(8,128)(2,1)S(1)}, bf16[512,384]{1,0:T(8,128)(2,1)S(1)}, u32[]{:S(2)}, u32[]{:S(2)}) collective-permute-start(bf16[512,384]{1,0:T(8,128)(2,1)S(1)} %get-tuple-element.311.refs_1_), channel_id=1, source_target_pairs={{0,2},{1,3},{2,0},{3,1},{4,6},{5,7},{6,4},{7,5},{8,10},{9,11},{10,... | collective-permute-start | bytes 1179656 | tf_op jit(solution)/shard_map/ppermute | solution.py:320
  176.1 18.6 %collective-permute-start.36 = (bf16[512,384]{1,0:T(8,128)(2,1)S(1)}, bf16[512,384]{1,0:T(8,128)(2,1)S(1)}, u32[]{:S(2)}, u32[]{:S(2)}) collective-permute-start(bf16[512,384]{1,0:T(8,128)(2,1)S(1)} %get-tuple-element.310.refs_0_), channel_id=1, source_target_pairs={{0,8},{1,9},{2,10},{3,11},{4,12},{5,13},{6,14},{7,15},{8,0},{9,1},... | collective-permute-start | bytes 1179656 | tf_op jit(solution)/shard_map/ppermute | solution.py:320
  195.4 27.4 %collective-permute-start.42 = (bf16[1024,384]{1,0:T(8,128)(2,1)S(1)}, bf16[1024,384]{1,0:T(8,128)(2,1)S(1)}, u32[]{:S(2)}, u32[]{:S(2)}) collective-permute-start(bf16[1024,384]{1,0:T(8,128)(2,1)S(1)} %get-tuple-element.326.refs_0_), channel_id=1, source_target_pairs={{0,4},{1,5},{2,6},{3,7},{4,0},{5,1},{6,2},{7,3},{8,12},{9,13},{10,... | collective-permute-start | bytes 2359304 | tf_op jit(solution)/shard_map/ppermute | solution.py:320
  196.9 28.1 %collective-permute-start.43 = (bf16[1024,384]{1,0:T(8,128)(2,1)S(1)}, bf16[1024,384]{1,0:T(8,128)(2,1)S(1)}, u32[]{:S(2)}, u32[]{:S(2)}) collective-permute-start(bf16[1024,384]{1,0:T(8,128)(2,1)S(1)} %get-tuple-element.327.refs_1_), channel_id=1, source_target_pairs={{0,8},{1,9},{2,10},{3,11},{4,12},{5,13},{6,14},{7,15},{8,0},{9,1},... | collective-permute-start | bytes 2359304 | tf_op jit(solution)/shard_map/ppermute | solution.py:320
  197.1 25.6 %collective-permute-start.44 = (bf16[1024,256]{1,0:T(8,128)(2,1)S(1)}, bf16[1024,256]{1,0:T(8,128)(2,1)S(1)}, u32[]{:S(2)}, u32[]{:S(2)}) collective-permute-start(bf16[1024,256]{1,0:T(8,128)(2,1)S(1)} %get-tuple-element.328.refs_2_), channel_id=1, source_target_pairs={{0,2},{1,3},{2,0},{3,1},{4,6},{5,7},{6,4},{7,5},{8,10},{9,11},{10,... | collective-permute-start | bytes 1572872 | tf_op jit(solution)/shard_map/ppermute | solution.py:320
  198.8 23.9 %collective-permute-start.45 = (bf16[192,1024]{1,0:T(8,128)(2,1)S(1)}, bf16[192,1024]{1,0:T(8,128)(2,1)S(1)}, u32[]{:S(2)}, u32[]{:S(2)}) collective-permute-start(bf16[192,1024]{1,0:T(8,128)(2,1)S(1)} %slice.237), channel_id=1, source_target_pairs={{0,16},{1,17},{2,18},{3,19},{4,20},{5,21},{6,22},{7,23},{8,24},{9,... | collective-permute-start | bytes 1179656 | tf_op jit(solution)/shard_map/ppermute | solution.py:326
  225.8 36.2 %collective-permute-start.50 = (bf16[2048,256]{1,0:T(8,128)(2,1)S(1)}, bf16[2048,256]{1,0:T(8,128)(2,1)S(1)}, u32[]{:S(2)}, u32[]{:S(2)}) collective-permute-start(bf16[2048,256]{1,0:T(8,128)(2,1)S(1)} %get-tuple-element.334.refs_2_), channel_id=1, source_target_pairs={{0,8},{1,9},{2,10},{3,11},{4,12},{5,13},{6,14},{7,15},{8,0},{9,1},... | collective-permute-start | bytes 3145736 | tf_op jit(solution)/shard_map/ppermute | solution.py:320
  226.6 35.7 %collective-permute-start.48 = (bf16[2048,384]{1,0:T(8,128)(2,1)S(1)}, bf16[2048,384]{1,0:T(8,128)(2,1)S(1)}, u32[]{:S(2)}, u32[]{:S(2)}) collective-permute-start(bf16[2048,384]{1,0:T(8,128)(2,1)S(1)} %get-tuple-element.332.refs_0_), channel_id=1, source_target_pairs={{0,2},{1,3},{2,0},{3,1},{4,6},{5,7},{6,4},{7,5},{8,10},{9,11},{10,... | collective-permute-start | bytes 4718600 | tf_op jit(solution)/shard_map/ppermute | solution.py:320
  227.9 35.4 %collective-permute-start.49 = (bf16[2048,384]{1,0:T(8,128)(2,1)S(1)}, bf16[2048,384]{1,0:T(8,128)(2,1)S(1)}, u32[]{:S(2)}, u32[]{:S(2)}) collective-permute-start(bf16[2048,384]{1,0:T(8,128)(2,1)S(1)} %get-tuple-element.333.refs_1_), channel_id=1, source_target_pairs={{0,4},{1,5},{2,6},{3,7},{4,0},{5,1},{6,2},{7,3},{8,12},{9,13},{10,... | collective-permute-start | bytes 4718600 | tf_op jit(solution)/shard_map/ppermute | solution.py:320
  232.3 29.6 %collective-permute-start.51 = (bf16[256,1024]{1,0:T(8,128)(2,1)S(1)}, bf16[256,1024]{1,0:T(8,128)(2,1)S(1)}, u32[]{:S(2)}, u32[]{:S(2)}) collective-permute-start(bf16[256,1024]{1,0:T(8,128)(2,1)S(1)} %pad_maximum_fusion.6), channel_id=1, source_target_pairs={{0,16},{1,17},{2,18},{3,19},{4,20},{5,21},{6,22},{7,23},{8,24},{9,... | collective-permute-start | bytes 1572872 | tf_op jit(solution)/shard_map/ppermute | solution.py:326
  234.1 27.7 %collective-permute-start.52 = (f32[3,1024]{1,0:T(4,128)S(1)}, f32[3,1024]{1,0:T(4,128)S(1)}, u32[]{:S(2)}, u32[]{:S(2)}) collective-permute-start(f32[3,1024]{1,0:T(4,128)S(1)} %fusion.69), channel_id=1, source_target_pairs={{0,8},{1,9},{2,10},{3,11},{4,12},{5,13},{6,14},{7,15},{8,0},{9,1},... | collective-permute-start | bytes 36872 | tf_op jit(solution)/shard_map/ppermute | solution.py:320
  263.4 8.4 %collective-permute-start.53 = (f32[2,512]{1,0:T(2,128)S(1)}, f32[2,512]{1,0:T(2,128)S(1)}, u32[]{:S(2)}, u32[]{:S(2)}) collective-permute-start(f32[2,512]{1,0:T(2,128)S(1)} %pad_maximum_fusion.11), channel_id=1, source_target_pairs={{0,16},{1,17},{2,18},{3,19},{4,20},{5,21},{6,22},{7,23},{8,24},{9,... | collective-permute-start | bytes 12296 | tf_op jit(solution)/shard_map/ppermute | solution.py:320
  277.4 29.0 %all-to-all-start.1 = ((bf16[8,128,512]{2,1,0:T(8,128)(2,1)}), bf16[8,128,512]{2,1,0:T(8,128)(2,1)S(1)}, u32[]{:S(2)}, u32[]{:S(2)}) async-start(bf16[8,128,512]{2,1,0:T(8,128)(2,1)} %shard_map.64), calls=%async_computation.1 | async-start | bytes 2097152 | tf_op jit(solution)/shard_map/all_to_all | solution.py:334
  281.1 23.7 %collective-permute-start.60 = (bf16[128,2048]{1,0:T(8,128)(2,1)S(1)}, bf16[128,2048]{1,0:T(8,128)(2,1)S(1)}, u32[]{:S(2)}, u32[]{:S(2)}) collective-permute-start(bf16[128,2048]{1,0:T(8,128)(2,1)S(1)} %get-tuple-element.391), channel_id=1, source_target_pairs={{0,16},{1,17},{2,18},{3,19},{4,20},{5,21},{6,22},{7,23},{8,24},{9,... | collective-permute-start | bytes 1572872 | tf_op jit(solution)/shard_map/ppermute | solution.py:326
  282.7 21.6 %collective-permute-start.59 = (f32[8,128]{1,0:T(8,128)S(1)}, f32[8,128]{1,0:T(8,128)S(1)}, u32[]{:S(2)}, u32[]{:S(2)}) collective-permute-start(f32[8,128]{1,0:T(8,128)S(1)} %add.193), channel_id=1, source_target_pairs={{0,16},{1,17},{2,18},{3,19},{4,20},{5,21},{6,22},{7,23},{8,24},{9,... | collective-permute-start | bytes 12296 | tf_op jit(solution)/shard_map/ppermute | solution.py:320
  (60 other events, 325.6 us)
